TPU v7x, 32 devices: a whole 2x2x4 slice. The times are simulated.
32 devices in a mesh: dir: 2 (over core), seq: 16 (over z, y, x).
Axes of the slice: x: 2, y: 2, z: 4, core: 2. Of those that a mesh axis runs over, the one named last changes fastest.
Arguments:
- queries: bfloat16 [2, 4, 1024, 4096], P('dir', None, 'seq'), may hold values from -35 to 35
- key_states: bfloat16 [2, 4, 1024, 4096], P('dir', None, 'seq'), may hold values from -6 to 6
- value_vectors: bfloat16 [2, 4, 1024, 4096], P('dir', None, 'seq'), may hold values from -6 to 6
- hypothesis_lengths: int32 [4, 64], replicated, may hold values from 1 to 256, 1024 in all within a row
- join_weight: bfloat16 [8192, 2, 1024], P('seq', None, 'dir'), may hold values from -0.0625 to 0.0625
Outputs:
- joined: bfloat16 [4, 1024, 1024], P(None, 'seq', 'dir')
All inputs are finite; a program needn't handle non-finite values.
Results may differ from a plain program's by a relative error of at most 0.0072.
Values may be sent and summed in bfloat16 or wider, within the bound.
A program may use at most 128 MiB of HBM per device.

v0:
```python
import math

import jax
import jax.numpy as jnp
from jax import lax
from jax.sharding import PartitionSpec as P

ATTENTION_HEADS = 32
LONGEST_TOKENS = 256


def swapped(array, axis, stride):
    return lax.ppermute(array, axis, [(i, i ^ 1 << stride) for i in range(lax.axis_size(axis))])


def hypothesis_tables(length_list, row_len):
    ends = jnp.cumsum(length_list)
    starts = ends - length_list
    places = jnp.arange(row_len, dtype=jnp.int32)
    inside = (places[:, None] >= starts[None, :]) & (places[:, None] < ends[None, :])
    first = jnp.sum(jnp.where(inside, starts[None, :], 0), axis=1)
    after = jnp.sum(jnp.where(inside, ends[None, :], 0), axis=1)
    mirror = first + after - 1 - places
    return (first, mirror)


def attend_group(query_row, k_row, v_row, first):
    row_len = query_row.shape[0]
    block_item = min(512, row_len)
    token_span = min(block_item + LONGEST_TOKENS, row_len)
    scale = 1.0 / math.sqrt(query_row.shape[2])

    def single_block(index):
        q_start = index * block_item
        k_start = jnp.maximum(q_start + block_item - token_span, 0)
        q_part = lax.dynamic_slice_in_dim(query_row, q_start, block_item, 0)
        k_part = lax.dynamic_slice_in_dim(k_row, k_start, token_span, 0)
        v_part = lax.dynamic_slice_in_dim(v_row, k_start, token_span, 0)
        scores = (
            jnp.einsum("qhc,khc->hqk", q_part, k_part, preferred_element_type=jnp.float32) * scale
        )
        q_places = q_start + jnp.arange(block_item, dtype=jnp.int32)
        k_places = k_start + jnp.arange(token_span, dtype=jnp.int32)
        starts = lax.dynamic_slice_in_dim(first, q_start, block_item, 0)
        allowed = (k_places[None, :] >= starts[:, None]) & (k_places[None, :] <= q_places[:, None])
        scores = jnp.where(allowed[None], scores, jnp.float32(-1e30))
        top = jnp.max(scores, axis=2, keepdims=True)
        raised = jnp.exp(scores - top)
        weights = (raised / jnp.sum(raised, axis=2, keepdims=True)).astype(jnp.bfloat16)
        return jnp.einsum(
            "hqk,khc->qhc", weights, v_part, preferred_element_type=jnp.float32
        ).astype(jnp.bfloat16)

    block_list = lax.map(single_block, jnp.arange(row_len // block_item, dtype=jnp.int32))
    return block_list.reshape(row_len, query_row.shape[1], query_row.shape[2])


def body(queries, key_states, value_vectors, hypothesis_lengths, join_weight):
    rows, piece, width = (queries.shape[1], queries.shape[2], queries.shape[3])
    devices = lax.axis_size("seq")
    groups = devices // rows
    head_width = width // ATTENTION_HEADS
    pair = width // groups
    heads_here = pair // head_width
    row_bits = rows.bit_length() - 1
    place = lax.axis_index("seq")
    row = place % rows
    row_len = devices * piece

    def regroup(states):
        states = states.reshape(rows, piece, groups, pair)
        return jnp.transpose(states, (2, 0, 1, 3)).reshape(groups * rows, piece, pair)

    q_all, k_all, v_all = (
        lax.all_to_all(regroup(queries[0]), "seq", split_axis=0, concat_axis=1, tiled=True),
        lax.all_to_all(regroup(key_states[0]), "seq", split_axis=0, concat_axis=1, tiled=True),
        lax.all_to_all(regroup(value_vectors[0]), "seq", split_axis=0, concat_axis=1, tiled=True),
    )
    block_rows = join_weight
    for bit in range(row_bits):
        partner = swapped(block_rows, "seq", bit)
        lower = place // 2**bit % 2 == 0
        block_rows = jnp.where(
            lower,
            jnp.concatenate([block_rows, partner], 0),
            jnp.concatenate([partner, block_rows], 0),
        )
    length_list = lax.dynamic_index_in_dim(hypothesis_lengths, row, 0, keepdims=False)
    first, mirror = hypothesis_tables(length_list, row_len)
    array_shape = (row_len, heads_here, head_width)
    context_vectors = attend_group(
        q_all.reshape(array_shape), k_all.reshape(array_shape), v_all.reshape(array_shape), first
    )
    other = swapped(context_vectors, "dir", 0)
    side = lax.axis_index("dir")
    left_side = jnp.where(side == 0, context_vectors, other)
    right_side = jnp.where(side == 0, other, context_vectors)
    right_side = jnp.take(right_side, mirror, axis=0)
    feature_rows = jnp.stack([left_side, right_side], axis=2).reshape(row_len, 2 * pair)
    columns = block_rows.shape[2]
    partial_value = jnp.dot(
        feature_rows, block_rows.reshape(2 * pair, 2 * columns), preferred_element_type=jnp.float32
    ).astype(jnp.bfloat16)
    arrived = lax.all_to_all(
        partial_value.reshape(devices, piece, 2 * columns),
        "seq",
        split_axis=0,
        concat_axis=0,
        tiled=True,
    )
    totals = jnp.sum(arrived.reshape(groups, rows, piece, 2 * columns).astype(jnp.float32), axis=0)
    joined = jax.nn.silu(totals[..., :columns]) * totals[..., columns:]
    return joined.astype(jnp.bfloat16)


def solution(mesh):
    return jax.shard_map(
        body,
        mesh=mesh,
        in_specs=(
            P("dir", None, "seq", None),
            P("dir", None, "seq", None),
            P("dir", None, "seq", None),
            P(),
            P("seq", None, "dir"),
        ),
        out_specs=P(None, "seq", "dir"),
        check_vma=False,
    )
```

profile of v0, /device:TPU:0, one launch (start us, length us, event | category | flops | bytes accessed | tf_op | source)
XLA Modules:
  0.0 326.1 jit_solution(14420199381214589765)
XLA Ops:
  0.0 3.3 %reshape_squeeze.9 = bf16[4,64,4,1024]{3,2,1,0:T(4,128)(2,1)S(1)} reshape(bf16[1,4,64,4096]{3,2,1,0:T(8,128)(2,1)} %param.9) | data formatting | bytes 4194304 | tf_op jit(solution)/shard_map/reshape;squeeze | solution.py:71
  3.3 2.0 copy.24
  5.3 8.3 %all-to-all-start = ((bf16[16,64,1024]{2,1,0:T(8,128)(2,1)}), bf16[16,64,1024]{2,1,0:T(8,128)(2,1)S(1)}, u32[]{:S(2)}, u32[]{:S(2)}) async-start(bf16[16,64,1024]{2,1,0:T(8,128)(2,1)} %bitcast.61), calls=%async_computation | async-start | bytes 4194304 | tf_op jit(solution)/shard_map/all_to_all | solution.py:77
  13.6 4.5 %reshape_squeeze.10 = bf16[4,64,4,1024]{3,2,1,0:T(4,128)(2,1)} reshape(bf16[1,4,64,4096]{3,2,1,0:T(8,128)(2,1)} %param.7) | data formatting | bytes 4194304 | tf_op jit(solution)/shard_map/reshape;squeeze | solution.py:71
  18.1 3.5 %copy.26 = bf16[4,4,64,1024]{3,2,1,0:T(8,128)(2,1)} copy(bf16[4,4,64,1024]{3,0,2,1:T(4,128)(2,1)} %bitcast.64) | data formatting | bytes 4194304 | tf_op jit(solution)/shard_map/transpose | solution.py:72
  21.7 35.0 %all-to-all-done = bf16[16,64,1024]{2,1,0:T(8,128)(2,1)S(1)} async-done(((bf16[16,64,1024]{2,1,0:T(8,128)(2,1)}), bf16[16,64,1024]{2,1,0:T(8,128)(2,1)S(1)}, u32[]{:S(2)}, u32[]{:S(2)}) %all-to-all-start) | async-done | bytes 2097184 | tf_op jit(solution)/shard_map/all_to_all | solution.py:77
  56.7 10.0 %all-to-all-start.1 = ((bf16[16,64,1024]{2,1,0:T(8,128)(2,1)}), bf16[16,64,1024]{2,1,0:T(8,128)(2,1)}, u32[]{:S(2)}, u32[]{:S(2)}) async-start(bf16[16,64,1024]{2,1,0:T(8,128)(2,1)} %bitcast.60), calls=%async_computation.1 | async-start | bytes 4194304 | tf_op jit(solution)/shard_map/all_to_all | solution.py:75
  66.7 4.5 %reshape_squeeze.11 = bf16[4,64,4,1024]{3,2,1,0:T(4,128)(2,1)} reshape(bf16[1,4,64,4096]{3,2,1,0:T(8,128)(2,1)} %param.8) | data formatting | bytes 4194304 | tf_op jit(solution)/shard_map/reshape;squeeze | solution.py:71
  71.2 3.5 %copy.27 = bf16[4,4,64,1024]{3,2,1,0:T(8,128)(2,1)} copy(bf16[4,4,64,1024]{3,0,2,1:T(4,128)(2,1)} %bitcast.65) | data formatting | bytes 4194304 | tf_op jit(solution)/shard_map/transpose | solution.py:72
  74.8 34.5 %all-to-all-done.1 = bf16[16,64,1024]{2,1,0:T(8,128)(2,1)} async-done(((bf16[16,64,1024]{2,1,0:T(8,128)(2,1)}), bf16[16,64,1024]{2,1,0:T(8,128)(2,1)}, u32[]{:S(2)}, u32[]{:S(2)}) %all-to-all-start.1) | async-done | bytes 2097184 | tf_op jit(solution)/shard_map/all_to_all | solution.py:75
  109.3 10.0 %all-to-all-start.2 = ((bf16[16,64,1024]{2,1,0:T(8,128)(2,1)}), bf16[16,64,1024]{2,1,0:T(8,128)(2,1)}, u32[]{:S(2)}, u32[]{:S(2)}) async-start(bf16[16,64,1024]{2,1,0:T(8,128)(2,1)} %bitcast.59), calls=%async_computation.2 | async-start | bytes 4194304 | tf_op jit(solution)/shard_map/all_to_all | solution.py:76
  122.2 43.5 %collective-permute-done.1 = bf16[512,2,512]{2,1,0:T(2,128)(2,1)} collective-permute-done((bf16[512,2,512]{2,1,0:T(2,128)(2,1)S(1)}, bf16[512,2,512]{2,1,0:T(2,128)(2,1)}, u32[]{:S(2)}, u32[]{:S(2)}) %collective-permute-start.1) | collective-permute-done | bytes 1048608 | tf_op jit(solution)/shard_map/ppermute | solution.py:13
  165.7 6.6 %broadcast_select_fusion = bf16[1024,2,512]{2,1,0:T(2,128)(2,1)} fusion(pred[]{:T(512)S(6)} %eq.16, bf16[512,2,512]{2,1,0:T(2,128)(2,1)} %collective-permute-done.1, bf16[512,2,512]{2,1,0:T(2,128)(2,1)S(1)} %copy-done.1), kind=kLoop, calls=%fused_computation.34 | loop fusion | flops 3145728 | bytes 4194305 | tf_op jit(solution)/shard_map/jit(_where)/select_n | solution.py:83
  174.0 2.0 copy.38
  176.0 3.5 %copy.39 = bf16[128,8,8,128]{3,2,1,0:T(8,128)(2,1)} copy(bf16[128,8,8,128]{3,1,2,0:T(8,128)(2,1)} %bitcast.28) | data formatting | bytes 4194304
  179.5 3.5 %copy.40 = bf16[128,8,8,128]{3,2,1,0:T(8,128)(2,1)} copy(bf16[128,8,8,128]{3,1,2,0:T(8,128)(2,1)} %bitcast.32) | data formatting | bytes 4194304
  183.1 51.0 %while.14 = (s32[]{:T(128)}, bf16[2,512,8,128]{3,2,1,0:T(8,128)(2,1)}, s32[2]{0:T(128)S(1)}, bf16[1024,8,128]{2,1,0:T(8,128)(2,1)}, s32[1024]{0:T(1024)S(1)}, /*...) while((s32[]{:T(128)}, ...), condition=%wide.region_5.6_spmd, body=%wide.region_2.5_spmd.sunk | while | flops 1637484544 | bytes 68993752 | solution.py:54
  186.0 3.3 %constant_dynamic-slice_fusion.6 = (bf16[768,8,128]{2,1,0:T(8,128)(2,1)S(1)}, bf16[768,8,128]{2,1,0:T(8,128)(2,1)}) fusion(bf16[1024,8,128]{2,1,0:T(8,128)(2,1)} %get-tuple-element.273, s32[]{:T(128)S(6)} %max.10, bf16[1024,8,128]{2,1,0:T(8,128)(2,1)} %get-tuple-element.270), kind=kLoop, calls=%fused_computation.20.clone.1 | loop fusion | bytes 6291460 | tf_op jit(solution)/shard_map/while/body/eval_jaxpr/dynamic_slice | solution.py:37
  191.1 8.5 %fusion.43 = (f32[8,512]{1,0:T(8,128)S(1)}, f32[8,512,768]{2,1,0:T(8,128)}) fusion(f32[8,512,768]{2,1,0:T(8,128)S(1)} %fusion.42, pred[512,768]{1,0:T(8,128)(4,1)S(1)} %compare_and_fusion.3), kind=kOutput, calls=%fused_computation.58.clone.1 | output fusion | flops 18875136 | bytes 25575424 | tf_op jit(solution)/shard_map/while/body/eval_jaxpr/sub | solution.py:48
  199.6 7.1 %fusion.44 = bf16[1,512,8,128]{1,3,2,0:T(8,128)(2,1)S(1)} fusion(f32[8,512,768]{2,1,0:T(8,128)} %get-tuple-element.240, f32[8,512]{1,0:T(8,128)S(1)} %get-tuple-element.241, bf16[768,8,128]{2,1,0:T(8,128)(2,1)} %get-tuple-element.242), kind=kOutput, calls=%fused_computation.15.clone.1 | convolution fusion | flops 812122112 | bytes 15220736 | tf_op jit(solution)/shard_map/while/body/eval_jaxpr/hqk,khc->qhc/dot_general | solution.py:50
  211.5 3.3 %constant_dynamic-slice_fusion.6 = (bf16[768,8,128]{2,1,0:T(8,128)(2,1)S(1)}, bf16[768,8,128]{2,1,0:T(8,128)(2,1)}) fusion(bf16[1024,8,128]{2,1,0:T(8,128)(2,1)} %get-tuple-element.273, s32[]{:T(128)S(6)} %max.10, bf16[1024,8,128]{2,1,0:T(8,128)(2,1)} %get-tuple-element.270), kind=kLoop, calls=%fused_computation.20.clone.1 | loop fusion | bytes 6291460 | tf_op jit(solution)/shard_map/while/body/eval_jaxpr/dynamic_slice | solution.py:37
  216.7 8.5 %fusion.43 = (f32[8,512]{1,0:T(8,128)S(1)}, f32[8,512,768]{2,1,0:T(8,128)}) fusion(f32[8,512,768]{2,1,0:T(8,128)S(1)} %fusion.42, pred[512,768]{1,0:T(8,128)(4,1)S(1)} %compare_and_fusion.3), kind=kOutput, calls=%fused_computation.58.clone.1 | output fusion | flops 18875136 | bytes 25575424 | tf_op jit(solution)/shard_map/while/body/eval_jaxpr/sub | solution.py:48
  225.1 7.1 %fusion.44 = bf16[1,512,8,128]{1,3,2,0:T(8,128)(2,1)S(1)} fusion(f32[8,512,768]{2,1,0:T(8,128)} %get-tuple-element.240, f32[8,512]{1,0:T(8,128)S(1)} %get-tuple-element.241, bf16[768,8,128]{2,1,0:T(8,128)(2,1)} %get-tuple-element.242), kind=kOutput, calls=%fused_computation.15.clone.1 | convolution fusion | flops 812122112 | bytes 15220736 | tf_op jit(solution)/shard_map/while/body/eval_jaxpr/hqk,khc->qhc/dot_general | solution.py:50
  237.1 2.4 maximum_select_fusion.2
  239.5 3.6 %copy.43 = bf16[128,8,2,512]{3,1,2,0:T(8,128)(2,1)} copy(bf16[128,8,2,512]{3,2,1,0:T(2,128)(2,1)} %bitcast.38) | data formatting | bytes 4194304
  243.2 2.3 select_bitcast_fusion
  245.5 4.9 %gather_fusion = bf16[1024,8,128]{2,1,0:T(8,128)(2,1)S(1)} fusion(bf16[1024,8,128]{2,1,0:T(8,128)(2,1)} %get-tuple-element.191, s32[1024]{0:T(1024)S(1)} %broadcast_clamp_fusion), kind=kCustom, calls=%fused_computation | custom fusion | bytes 4198400 | tf_op jit(solution)/shard_map/jit(_take)/gather | solution.py:98
  250.5 3.7 %bitcast_select_fusion = bf16[1024,8,1,128]{3,1,0,2:T(8,128)(2,1)S(1)} fusion(bf16[1024,8,128]{2,1,0:T(8,128)(2,1)S(1)} %gather_fusion, pred[1024]{0:T(1024)(128)(4,1)S(1)} %get-tuple-element.184), kind=kLoop, calls=%fused_computation.37 | loop fusion | flops 1048576 | bytes 4195328 | tf_op jit(solution)/shard_map/jit(_take)/select_n | solution.py:98
  254.2 2.3 pad_maximum_fusion
  256.5 6.8 %copy.32 = bf16[1024,8,2,128]{0,3,2,1:T(8,128)(2,1)} copy(bf16[1024,8,2,128]{3,1,0,2:T(8,128)(2,1)} %pad_maximum_fusion) | data formatting | bytes 8388608 | tf_op jit(solution)/shard_map/stack | solution.py:99
  263.4 8.1 %fusion.25 = bf16[1024,1024]{1,0:T(8,128)(2,1)S(1)} fusion(bf16[1024,2048]{0,1:T(8,128)(2,1)} %bitcast.69, bf16[1024,1024]{1,0:T(8,128)(2,1)} %bitcast.70, bf16[1024,1024]{1,0:T(8,128)(2,1)S(1)} %copy-done.2, pred[]{:T(512)S(6)} %eq.15), kind=kOutput, calls=%fused_computation.40 | convolution fusion | flops 4314890240 | bytes 10485761 | tf_op jit(solution)/shard_map/dot_general | solution.py:101
  271.4 53.4 %all_to_all.32 = bf16[16,64,1024]{2,1,0:T(8,128)(2,1)S(1)} all-to-all(bf16[16,64,1024]{2,1,0:T(8,128)(2,1)S(1)} %bitcast.71), channel_id=1, replica_groups=mesh['dir'=2,'seq'=16] {'seq'}, dimensions={0} | all-to-all | bytes 4194304 | tf_op jit(solution)/shard_map/all_to_all | solution.py:104
  (51 shorter events, 20.9 us)
Async XLA Ops:
  5.3 51.4 %all-to-all-start = ((bf16[16,64,1024]{2,1,0:T(8,128)(2,1)}), bf16[16,64,1024]{2,1,0:T(8,128)(2,1)S(1)}, u32[]{:S(2)}, u32[]{:S(2)}) async-start(bf16[16,64,1024]{2,1,0:T(8,128)(2,1)} %bitcast.61), calls=%async_computation | async-start | bytes 4194304 | tf_op jit(solution)/shard_map/all_to_all | solution.py:77
  56.7 52.6 %all-to-all-start.1 = ((bf16[16,64,1024]{2,1,0:T(8,128)(2,1)}), bf16[16,64,1024]{2,1,0:T(8,128)(2,1)}, u32[]{:S(2)}, u32[]{:S(2)}) async-start(bf16[16,64,1024]{2,1,0:T(8,128)(2,1)} %bitcast.60), calls=%async_computation.1 | async-start | bytes 4194304 | tf_op jit(solution)/shard_map/all_to_all | solution.py:75
  109.3 10.0 %copy-start.1 = (bf16[512,2,512]{2,1,0:T(2,128)(2,1)S(1)}, bf16[512,2,512]{2,1,0:T(2,128)(2,1)}, u32[]{:S(2)}) copy-start(bf16[512,2,512]{2,1,0:T(2,128)(2,1)} %param.11) | copy-start | bytes 3145732
  109.3 11.9 %copy-start.5 = (s32[4,64]{1,0:T(4,128)S(1)}, s32[4,64]{1,0:T(4,128)}, u32[]{:S(2)}) copy-start(s32[4,64]{1,0:T(4,128)} %param.10) | copy-start | bytes 3076
  109.3 70.3 %all-to-all-start.2 = ((bf16[16,64,1024]{2,1,0:T(8,128)(2,1)}), bf16[16,64,1024]{2,1,0:T(8,128)(2,1)}, u32[]{:S(2)}, u32[]{:S(2)}) async-start(bf16[16,64,1024]{2,1,0:T(8,128)(2,1)} %bitcast.59), calls=%async_computation.2 | async-start | bytes 4194304 | tf_op jit(solution)/shard_map/all_to_all | solution.py:76
  119.3 46.5 %collective-permute-start.1 = (bf16[512,2,512]{2,1,0:T(2,128)(2,1)S(1)}, bf16[512,2,512]{2,1,0:T(2,128)(2,1)}, u32[]{:S(2)}, u32[]{:S(2)}) collective-permute-start(bf16[512,2,512]{2,1,0:T(2,128)(2,1)S(1)} %copy-done.1), channel_id=1, source_target_pairs={{0,1},{1,0},{2,3},{3,2},{4,5},{5,4},{6,7},{7,6},{8,9},{9,8},{10,11... | collective-permute-start | bytes 3145736 | tf_op jit(solution)/shard_map/ppermute | solution.py:13
  172.3 67.2 %collective-permute-start.2 = (bf16[1024,2,512]{2,1,0:T(2,128)(2,1)}, bf16[1024,2,512]{2,1,0:T(2,128)(2,1)}, u32[]{:S(2)}, u32[]{:S(2)}) collective-permute-start(bf16[1024,2,512]{2,1,0:T(2,128)(2,1)} %broadcast_select_fusion), channel_id=1, source_target_pairs={{0,2},{1,3},{2,0},{3,1},{4,6},{5,7},{6,4},{7,5},{8,10},{9,11},{10,... | collective-permute-start | bytes 6291464 | tf_op jit(solution)/shard_map/ppermute | solution.py:13
  234.1 1.5 copy-start.4
  234.1 9.1 %collective-permute-start = (bf16[1024,8,128]{2,1,0:T(8,128)(2,1)}, bf16[1024,8,128]{2,1,0:T(8,128)(2,1)S(1)}, u32[]{:S(2)}, u32[]{:S(2)}) collective-permute-start(bf16[1024,8,128]{2,1,0:T(8,128)(2,1)} %bitcast.72), channel_id=1, source_target_pairs={{0,16},{16,0},{1,17},{17,1},{2,18},{18,2},{3,19},{19,3},{4,20},{20... | collective-permute-start | bytes 6291464 | tf_op jit(solution)/shard_map/ppermute | solution.py:13
  239.5 3.6 %copy-start.3 = (bf16[2,512,8,128]{3,2,1,0:T(8,128)(2,1)S(1)}, bf16[2,512,8,128]{3,2,1,0:T(8,128)(2,1)}, u32[]{:S(2)}) copy-start(bf16[2,512,8,128]{3,2,1,0:T(8,128)(2,1)} %get-tuple-element.146) | copy-start | bytes 6291460
  250.4 3.8 %copy-start = (bf16[1024,8,1,128]{3,1,0,2:T(8,128)(2,1)S(1)}, bf16[1024,8,1,128]{3,1,0,2:T(8,128)(2,1)}, u32[]{:S(2)}) copy-start(bf16[1024,8,1,128]{3,1,0,2:T(8,128)(2,1)} %get-tuple-element.190) | copy-start | bytes 6291460
  256.5 6.8 %copy-start.2 = (bf16[1024,1024]{1,0:T(8,128)(2,1)S(1)}, bf16[1024,1024]{1,0:T(8,128)(2,1)}, u32[]{:S(2)}) copy-start(bf16[1024,1024]{1,0:T(8,128)(2,1)} %maximum_select_fusion.2) | copy-start | bytes 6291460
where the time goes:
time: 327 us; the launch traced here: 326 us
  waiting for transfers between devices  113 us (35%)
  local copies, waits for them, and re-layouts  63 us (19%)
  blocking collectives  53.4 us (16%)
  other arithmetic  37.4 us (11%)
  starting transfers between devices  31.9 us (10%)
  matrix products  26 us (8%)
    all_to_all x1, blocking collectives, body(): lax.all_to_all(partial_value.reshape(devices, piece, 2 * columns), 'seq',...  53.4 us
    ppermute x3, waiting for transfers between devices, swapped(): lax.ppermute(array, axis, [(i, i ^ 1 << stride) for i in range(lax.axis_s...  43.5 us
    all_to_all x1, waiting for transfers between devices, body(): lax.all_to_all(regroup(value_vectors[0]), 'seq', split_axis=0, concat_axi...  35 us
    all_to_all x1, waiting for transfers between devices, body(): lax.all_to_all(regroup(queries[0]), 'seq', split_axis=0, concat_axis=1, t...  34.5 us
    sub x2, other arithmetic, single_block(): raised = jnp.exp(scores - top)  17 us
    unnamed x18, local copies, waits for them, and re-layouts  15.6 us
    dot_general x2, matrix products, single_block(): jnp.einsum('hqk,khc->qhc', weights, v_part, preferred_element_type=jnp.fl...  14.3 us
    another operation x3, local copies, waits for them, and re-layouts, regroup(): states = states.reshape(rows, piece, groups, pair)  12.3 us
  transfers between devices with their start and end apart: 6, of which 3 were waited for; matrix products, arithmetic and copies ran while one was open for 28% of the time, Pallas kernels for 0%

commit v1 on v0

--- a/solution.py
+++ b/solution.py
@@ -1,12 +1,16 @@
+import functools
 import math
 
 import jax
 import jax.numpy as jnp
 from jax import lax
+from jax.experimental import pallas as pl
+from jax.experimental.pallas import tpu as pltpu
 from jax.sharding import PartitionSpec as P
 
 ATTENTION_HEADS = 32
 LONGEST_TOKENS = 256
+PACKED_ROWS = 4
 
 
 def swapped(array, axis, stride):
@@ -113,9 +117,284 @@
     return joined.astype(jnp.bfloat16)
 
 
+def pair_kernel(
+    geometry, first_ref, source_ref, q_ref, k_ref, v_ref, weight_ref, out_ref,
+    states, weights, raw, feats, moves, bias, partials, arrived,
+    send_sem, recv_sem, local_sem, wsend_sem, wrecv_sem, wlocal_sem,
+    csend_sem, crecv_sem, psend_sem, precv_sem,
+):
+    devices, rows, groups, piece, head_width, chunks = geometry
+    side = lax.axis_index("dir")
+    me = lax.axis_index("seq")
+    wide = 2 * head_width
+    pair = chunks * wide
+    row_len = devices * piece
+    block = LONGEST_TOKENS
+    blocks = row_len // block
+    per_block = block // piece
+    scale = 1.0 / math.sqrt(head_width)
+    my_row = lax.rem(me, rows)
+    my_group = lax.div(me, rows)
+
+    def at(peer):
+        return {"device_id": (side, peer), "device_id_type": pl.DeviceIdType.MESH}
+
+    across = {"device_id": (1 - side, me), "device_id_type": pl.DeviceIdType.MESH}
+
+    barrier = pltpu.get_barrier_semaphore()
+
+    def greet(step, carry):
+        pl.semaphore_signal(barrier, inc=1, **at(lax.rem(me + step, devices)))
+        return carry
+
+    lax.fori_loop(1, devices, greet, 0)
+    pl.semaphore_signal(barrier, inc=1, **across)
+    pl.semaphore_wait(barrier, devices)
+
+    def own_piece(chunk, index, ref):
+        return pltpu.make_async_copy(
+            ref.at[0, my_row, :, pl.ds(pl.multiple_of(my_group * pair + chunk * wide, wide), wide)],
+            states.at[chunk, index, pl.ds(pl.multiple_of(me * piece, piece), piece), :],
+            local_sem.at[chunk],
+        )
+
+    def send_chunk(chunk, carry):
+        def send_to(step, inner):
+            peer = lax.rem(me + step, devices)
+            row, group = lax.rem(peer, rows), lax.div(peer, rows)
+            column = pl.multiple_of(group * pair + chunk * wide, wide)
+            for index, ref in enumerate((q_ref, k_ref, v_ref)):
+                pltpu.make_async_remote_copy(
+                    src_ref=ref.at[0, row, :, pl.ds(column, wide)],
+                    dst_ref=states.at[chunk, index, pl.ds(pl.multiple_of(me * piece, piece), piece), :],
+                    send_sem=send_sem.at[chunk],
+                    recv_sem=recv_sem.at[chunk],
+                    **at(peer),
+                ).start()
+            return inner
+
+        lax.fori_loop(1, devices, send_to, 0)
+        for index, ref in enumerate((q_ref, k_ref, v_ref)):
+            own_piece(chunk, index, ref).start()
+        return carry
+
+    lax.fori_loop(0, chunks, send_chunk, 0)
+
+    def send_weights(step, carry):
+        peer = my_group * rows + lax.rem(my_row + step, rows)
+        pltpu.make_async_remote_copy(
+            src_ref=weight_ref,
+            dst_ref=weights.at[my_row],
+            send_sem=wsend_sem,
+            recv_sem=wrecv_sem,
+            **at(peer),
+        ).start()
+        return carry
+
+    lax.fori_loop(1, rows, send_weights, 0)
+    own_weights = pltpu.make_async_copy(weight_ref, weights.at[my_row], wlocal_sem)
+    own_weights.start()
+
+    def tables(index, carry):
+        start = pl.multiple_of(index * block, block)
+        k_start = jnp.maximum(index - 1, 0) * block
+        first = first_ref[pl.ds(start, block), :]
+        source = source_ref[pl.ds(start, block), :]
+        k_places = k_start + lax.broadcasted_iota(jnp.int32, (block, 2 * block), 1)
+        q_places = start + lax.broadcasted_iota(jnp.int32, (block, 2 * block), 0)
+        allowed = (k_places >= first) & (k_places <= q_places)
+        bias[index] = jnp.where(allowed, jnp.float32(0), jnp.float32(-1e30))
+        places = lax.broadcasted_iota(jnp.int32, (block, row_len), 1)
+        moves[pl.ds(start, block), :] = jnp.where(places == source, 1.0, 0.0).astype(jnp.bfloat16)
+        return carry
+
+    lax.fori_loop(0, blocks, tables, 0)
+
+    def exchange(chunk, head):
+        column = pl.multiple_of((2 * head + side) * head_width, head_width)
+        there = feats.at[chunk, :, pl.ds(column, head_width)]
+        return pltpu.make_async_remote_copy(
+            src_ref=there,
+            dst_ref=there,
+            send_sem=csend_sem.at[chunk, head],
+            recv_sem=crecv_sem.at[chunk, head],
+            **across,
+        )
+
+    def work_chunk(chunk, carry):
+        others = states.at[chunk, :, pl.ds(0, row_len - piece), :]
+        pltpu.make_async_copy(others, others, recv_sem.at[chunk]).wait()
+        mine = states.at[chunk, :, pl.ds(0, piece), :]
+        pltpu.make_async_copy(mine, mine, local_sem.at[chunk]).wait()
+
+        def attend(index, inner):
+            start = pl.multiple_of(index * block, block)
+            k_start = pl.multiple_of(jnp.maximum(index - 1, 0) * block, block)
+            for head in range(2):
+                lanes = slice(head * head_width, (head + 1) * head_width)
+                q_part = states[chunk, 0, pl.ds(start, block), lanes]
+                k_part = states[chunk, 1, pl.ds(k_start, 2 * block), lanes]
+                v_part = states[chunk, 2, pl.ds(k_start, 2 * block), lanes]
+                scores = lax.dot_general(
+                    q_part, k_part, (((1,), (1,)), ((), ())), preferred_element_type=jnp.float32
+                )
+                scores = scores * scale + bias[index]
+                raised = jnp.exp(scores - jnp.max(scores, axis=1, keepdims=True))
+                share = 1.0 / jnp.sum(raised, axis=1, keepdims=True)
+                raw[pl.ds(start, block), lanes] = jnp.dot(
+                    (raised * share).astype(jnp.bfloat16), v_part, preferred_element_type=jnp.float32
+                ).astype(jnp.bfloat16)
+            return inner
+
+        lax.fori_loop(0, blocks, attend, 0)
+
+        def mirror(index, inner):
+            start = pl.multiple_of(index * block, block)
+            moved = jnp.dot(
+                moves[pl.ds(start, block), :], raw[...], preferred_element_type=jnp.float32
+            ).astype(jnp.bfloat16)
+            for head in range(2):
+                column = pl.multiple_of((2 * head + side) * head_width, head_width)
+                feats[chunk, pl.ds(start, block), pl.ds(column, head_width)] = moved[
+                    :, head * head_width : (head + 1) * head_width
+                ]
+            return inner
+
+        lax.fori_loop(0, blocks, mirror, 0)
+        for head in range(2):
+            exchange(chunk, head).start()
+        return carry
+
+    lax.fori_loop(0, chunks, work_chunk, 0)
+
+    gathered = weights.at[pl.ds(0, rows - 1)]
+    pltpu.make_async_copy(gathered, gathered, wrecv_sem).wait()
+    own_weights.wait()
+
+    def arrive(chunk, carry):
+        for head in range(2):
+            column = pl.multiple_of((2 * head + 1 - side) * head_width, head_width)
+            there = feats.at[chunk, :, pl.ds(column, head_width)]
+            pltpu.make_async_copy(there, there, crecv_sem.at[chunk, head]).wait()
+        return carry
+
+    lax.fori_loop(0, chunks, arrive, 0)
+
+    def join(step, carry):
+        index = lax.rem(lax.div(me, per_block) + 2 + step, blocks)
+        start = pl.multiple_of(index * block, block)
+        total = jnp.dot(
+            feats[0, pl.ds(start, block), :], weights[0], preferred_element_type=jnp.float32
+        )
+        for chunk in range(1, chunks):
+            total = total + jnp.dot(
+                feats[chunk, pl.ds(start, block), :], weights[chunk], preferred_element_type=jnp.float32
+            )
+        rounded = total.astype(jnp.bfloat16)
+        for part in range(per_block):
+            peer = index * per_block + part
+            partials[peer] = rounded[part * piece : (part + 1) * piece, :]
+
+            @pl.when(peer != me)
+            def _():
+                pltpu.make_async_remote_copy(
+                    src_ref=partials.at[peer],
+                    dst_ref=arrived.at[me],
+                    send_sem=psend_sem,
+                    recv_sem=precv_sem,
+                    **at(peer),
+                ).start()
+
+        return carry
+
+    lax.fori_loop(0, blocks, join, 0)
+    arrived[me] = partials[me]
+    incoming = arrived.at[pl.ds(0, devices - 1)]
+    pltpu.make_async_copy(incoming, incoming, precv_sem).wait()
+    columns = out_ref.shape[2]
+    for row in range(rows):
+        total = arrived[row].astype(jnp.float32)
+        for group in range(1, groups):
+            total = total + arrived[group * rows + row].astype(jnp.float32)
+        gate, up = total[:, :columns], total[:, columns:]
+        out_ref[row] = (gate / (1.0 + jnp.exp(-gate)) * up).astype(jnp.bfloat16)
+
+    def finish(chunk, carry):
+        others = states.at[chunk, :, pl.ds(0, row_len - piece), :]
+        pltpu.make_async_copy(others, others, send_sem.at[chunk]).wait()
+        for head in range(2):
+            exchange(chunk, head).wait_send()
+        return carry
+
+    lax.fori_loop(0, chunks, finish, 0)
+    pltpu.make_async_copy(gathered, gathered, wsend_sem).wait()
+    pltpu.make_async_copy(incoming, incoming, psend_sem).wait()
+
+
+def fused_body(queries, key_states, value_vectors, hypothesis_lengths, join_weight):
+    rows, piece, width = (queries.shape[1], queries.shape[2], queries.shape[3])
+    devices = lax.axis_size("seq")
+    groups = devices // rows
+    head_width = width // ATTENTION_HEADS
+    pair = width // groups
+    wide = 2 * head_width
+    chunks = pair // wide
+    row_len = devices * piece
+    blocks = row_len // LONGEST_TOKENS
+    weight_rows, _, columns = join_weight.shape
+    length_list = lax.dynamic_index_in_dim(
+        hypothesis_lengths, lax.axis_index("seq") % rows, 0, keepdims=False
+    )
+    first, mirror = hypothesis_tables(length_list, row_len)
+    places = jnp.arange(row_len, dtype=jnp.int32)
+    source = jnp.where(lax.axis_index("dir") == 0, places, mirror)
+    geometry = (devices, rows, groups, piece, head_width, chunks)
+    return pl.pallas_call(
+        functools.partial(pair_kernel, geometry),
+        out_shape=jax.ShapeDtypeStruct((rows, piece, columns), jnp.bfloat16),
+        in_specs=[pl.BlockSpec(memory_space=pltpu.VMEM)] * 2 + [pl.BlockSpec(memory_space=pl.ANY)] * 4,
+        out_specs=pl.BlockSpec(memory_space=pltpu.VMEM),
+        scratch_shapes=[
+            pltpu.VMEM((chunks, 3, row_len, wide), jnp.bfloat16),
+            pltpu.VMEM((chunks, weight_rows, 2 * columns), jnp.bfloat16),
+            pltpu.VMEM((row_len, wide), jnp.bfloat16),
+            pltpu.VMEM((chunks, row_len, 2 * wide), jnp.bfloat16),
+            pltpu.VMEM((row_len, row_len), jnp.bfloat16),
+            pltpu.VMEM((blocks, LONGEST_TOKENS, 2 * LONGEST_TOKENS), jnp.float32),
+            pltpu.VMEM((devices, piece, 2 * columns), jnp.bfloat16),
+            pltpu.VMEM((devices, piece, 2 * columns), jnp.bfloat16),
+            pltpu.SemaphoreType.DMA((chunks,)),
+            pltpu.SemaphoreType.DMA((chunks,)),
+            pltpu.SemaphoreType.DMA((chunks,)),
+            pltpu.SemaphoreType.DMA,
+            pltpu.SemaphoreType.DMA,
+            pltpu.SemaphoreType.DMA,
+            pltpu.SemaphoreType.DMA((chunks, 2)),
+            pltpu.SemaphoreType.DMA((chunks, 2)),
+            pltpu.SemaphoreType.DMA,
+            pltpu.SemaphoreType.DMA,
+        ],
+        compiler_params=pltpu.CompilerParams(
+            collective_id=0, has_side_effects=True, vmem_limit_bytes=48 * 1024 * 1024
+        ),
+    )(
+        first[:, None],
+        source[:, None],
+        queries,
+        key_states,
+        value_vectors,
+        join_weight.reshape(weight_rows, 2 * columns),
+    )
+
+
+def fits_kernel(mesh):
+    groups = mesh.shape["seq"] // PACKED_ROWS
+    return ATTENTION_HEADS // groups == 2 * PACKED_ROWS
+
+
 def solution(mesh):
     return jax.shard_map(
-        body,
+        fused_body if fits_kernel(mesh) else body,
         mesh=mesh,
         in_specs=(
             P("dir", None, "seq", None),

time: 327 us -> 199 us (0.61)
  the two profiles are of different devices: /device:TPU:0 before, /device:TPU:23 now
where the time goes in v1:
time: 199 us; the launch traced here: 198 us
  Pallas kernels  194 us (97%)
  local copies, waits for them, and re-layouts  3.57 us (2%)
    pallas_call x1, Pallas kernels, fused_body(): pl.pallas_call(functools.partial(pair_kernel, geometry), out_shape=jax.Sh...  194 us

profile of v1, /device:TPU:23, one launch (start us, length us, event | category | flops | bytes accessed | tf_op | source)
XLA Modules:
  0.0 198.3 jit_solution(11754526698830876489)
XLA Ops:
  0.0 0.7 fusion.2
  0.7 0.1 copy.11
  0.8 0.1 reduce-window.4
  0.9 0.1 reduce
  1.0 0.7 fusion.1
  1.7 0.1 select_reduce_fusion
  1.8 0.2 copy.14.first_ref
  2.1 0.0 copy-start
  2.1 0.2 copy.13
  2.3 0.1 subtract_select_fusion.source_ref
  2.4 1.6 copy.15
  4.0 0.0 copy-done
  4.1 193.6 %shard_map.55 = bf16[4,64,512]{2,1,0:T(8,128)(2,1)S(1)} custom-call(s32[1024,1]{1,0:T(8,128)S(1)} %copy.14.first_ref, s32[1024,1]{1,0:T(8,128)S(1)} %subtract_select_fusion.source_ref, bf16[1,4,64,4096]{3,2,1,0:T(8,128)(2,1)S(1)} %copy-done, bf16[1,4,64,4096]{3,2,1,0:T(8,128)(2,1)} %k_ref.1, bf16[1,4,64,4096]{3,2,1,0:T(8,128)(2,1)} %v_ref.1, ...), custom_call_target="tpu_custom_call" | custom-call | tf_op jit(solution)/shard_map/pallas_call | solution.py:352
  197.6 0.7 copy.17
Async XLA Ops:
  2.1 2.0 %copy-start = (bf16[1,4,64,4096]{3,2,1,0:T(8,128)(2,1)S(1)}, bf16[1,4,64,4096]{3,2,1,0:T(8,128)(2,1)}, u32[]{:S(2)}) copy-start(bf16[1,4,64,4096]{3,2,1,0:T(8,128)(2,1)} %q_ref.1) | copy-start | bytes 6291460

commit v2 on v0

--- a/solution.py
+++ b/solution.py
@@ -1,12 +1,16 @@
+import functools
 import math
 
 import jax
 import jax.numpy as jnp
 from jax import lax
+from jax.experimental import pallas as pl
+from jax.experimental.pallas import tpu as pltpu
 from jax.sharding import PartitionSpec as P
 
 ATTENTION_HEADS = 32
 LONGEST_TOKENS = 256
+PACKED_ROWS = 4
 
 
 def swapped(array, axis, stride):
@@ -113,9 +117,524 @@
     return joined.astype(jnp.bfloat16)
 
 
+def pair_kernel(
+    geometry, table_ref, q_ref, k_ref, v_ref, weight_ref, out_ref,
+    states, queries_up, raw, own, up_from, up_into, down_from, down_into,
+    own_stats, up_stats_from, up_stats_into, down_stats_from, down_stats_into,
+    weights, feats, sums, partials, arrived, own_moves, up_moves, down_moves, own_bias, up_bias,
+    send_sem, recv_sem, local_sem, qsend_sem, qrecv_sem, usend_sem, urecv_sem, dsend_sem, drecv_sem,
+    wsend_sem, wrecv_sem, wlocal_sem, csend_sem, crecv_sem, psend_sem, precv_sem,
+):
+    planes, rows, members, piece, head_width, chunks = geometry
+    side = lax.axis_index("dir")
+    me = lax.axis_index("seq")
+    plane, member = lax.div(me, members), lax.rem(me, members)
+    wide = 2 * head_width
+    span = members * piece
+    scale = 1.0 / math.sqrt(head_width)
+    has_up, has_down = plane < planes - 1, plane > 0
+
+    def at(peer):
+        return {"device_id": (side, peer), "device_id_type": pl.DeviceIdType.MESH}
+
+    def beside(step):
+        return at(plane * members + lax.rem(member + step, members))
+
+    above, below = at(me + members), at(me - members)
+    across = {"device_id": (1 - side, me), "device_id_type": pl.DeviceIdType.MESH}
+
+    barrier = pltpu.get_barrier_semaphore()
+    for step in range(1, members):
+        pl.semaphore_signal(barrier, inc=1, **beside(step))
+    pl.semaphore_signal(barrier, inc=1, **across)
+
+    @pl.when(has_up)
+    def _():
+        pl.semaphore_signal(barrier, inc=1, **above)
+
+    @pl.when(has_down)
+    def _():
+        pl.semaphore_signal(barrier, inc=1, **below)
+
+    pl.semaphore_wait(barrier, members + jnp.where(has_up, 1, 0) + jnp.where(has_down, 1, 0))
+
+    def weight_copy(shard, source, way, target):
+        return pltpu.make_async_remote_copy(
+            src_ref=source,
+            dst_ref=weights.at[shard],
+            send_sem=wsend_sem.at[way, shard],
+            recv_sem=wrecv_sem.at[shard],
+            **target,
+        )
+
+    def input_column(chunk, owner):
+        return pl.ds(pl.multiple_of((chunk * members + owner) * wide, wide), wide)
+
+    def landing(chunk, index):
+        return states.at[chunk, index, :, pl.ds(pl.multiple_of(member * piece, piece), piece), :]
+
+    def send_chunk(chunk, carry):
+        for step in range(1, members):
+            owner = lax.rem(member + step, members)
+            for index, ref in enumerate((q_ref, k_ref, v_ref)):
+                pltpu.make_async_remote_copy(
+                    src_ref=ref.at[0, :, :, input_column(chunk, owner)],
+                    dst_ref=landing(chunk, index),
+                    send_sem=send_sem.at[chunk],
+                    recv_sem=recv_sem.at[chunk],
+                    **beside(step),
+                ).start()
+        for index, ref in enumerate((q_ref, k_ref, v_ref)):
+            pltpu.make_async_copy(
+                ref.at[0, :, :, input_column(chunk, member)], landing(chunk, index), local_sem.at[chunk]
+            ).start()
+        return carry
+
+    lax.fori_loop(0, chunks, send_chunk, 0)
+
+    @pl.when(has_up)
+    def _():
+        weight_copy(plane, weight_ref, 0, above).start()
+
+    @pl.when(has_down)
+    def _():
+        weight_copy(plane, weight_ref, 1, below).start()
+
+    own_weights = pltpu.make_async_copy(weight_ref, weights.at[plane], wlocal_sem)
+    own_weights.start()
+
+    def relay_weights(step):
+        @pl.when(plane - step >= 0)
+        def _():
+            shard = weights.at[plane - step]
+            pltpu.make_async_copy(shard, shard, wrecv_sem.at[plane - step]).wait()
+
+            @pl.when(has_up)
+            def _():
+                weight_copy(plane - step, shard, 0, above).start()
+
+        @pl.when(plane + step < planes)
+        def _():
+            shard = weights.at[plane + step]
+            pltpu.make_async_copy(shard, shard, wrecv_sem.at[plane + step]).wait()
+
+            @pl.when(has_down)
+            def _():
+                weight_copy(plane + step, shard, 1, below).start()
+
+    @pl.when(jnp.logical_not(has_up))
+    def _():
+        queries_up[...] = jnp.zeros_like(queries_up)
+
+    @pl.when(jnp.logical_not(has_down))
+    def _():
+        up_into[...] = jnp.zeros_like(up_into)
+        up_stats_into[...] = jnp.zeros_like(up_stats_into)
+
+    gets_down = jnp.logical_and(has_up, side == 1)
+    gives_down = jnp.logical_and(has_down, side == 1)
+
+    @pl.when(jnp.logical_not(gets_down))
+    def _():
+        down_into[...] = jnp.zeros_like(down_into)
+        down_stats_into[...] = jnp.zeros_like(down_stats_into)
+
+    def tables(row, carry):
+        table = table_ref[row]
+        k_places = lax.broadcasted_iota(jnp.int32, (span, span), 1)
+        q_places = lax.broadcasted_iota(jnp.int32, (span, span), 0)
+        places = lax.broadcasted_iota(jnp.int32, (span, 2 * span), 1)
+        allowed = (k_places >= table[:, 0:1]) & (k_places <= q_places)
+        own_bias[row] = jnp.where(allowed, jnp.float32(0), jnp.float32(-1e30))
+        up_bias[row] = jnp.where(k_places >= table[:, 1:2], jnp.float32(0), jnp.float32(-1e30))
+        own_moves[row] = jnp.where(places == table[:, 2:3], 1.0, 0.0).astype(jnp.bfloat16)
+        up_moves[row] = jnp.where(places == table[:, 3:4], 1.0, 0.0).astype(jnp.bfloat16)
+        down_moves[row] = jnp.where(k_places == table[:, 4:5], 1.0, 0.0).astype(jnp.bfloat16)
+        return carry
+
+    lax.fori_loop(0, rows, tables, 0)
+
+    def attend(chunk, part, q_of, bias_ref):
+        def attend_row(row, inner):
+            lane = lax.broadcasted_iota(jnp.int32, (span, head_width), 1) - row * 8
+            stats = jnp.where(lane == 6, jnp.float32(1), jnp.float32(0))
+            for head in range(2):
+                lanes = slice(head * head_width, (head + 1) * head_width)
+                scores = lax.dot_general(
+                    q_of(row, lanes),
+                    states[chunk, 1, row, :, lanes],
+                    (((1,), (1,)), ((), ())),
+                    preferred_element_type=jnp.float32,
+                )
+                scores = scores * scale + bias_ref[row]
+                top = jnp.max(scores, axis=1, keepdims=True)
+                raised = jnp.exp(scores - top)
+                total = jnp.sum(raised, axis=1, keepdims=True)
+                raw[chunk, row, part * span : (part + 1) * span, lanes] = jnp.dot(
+                    (raised * (1.0 / total)).astype(jnp.bfloat16),
+                    states[chunk, 2, row, :, lanes],
+                    preferred_element_type=jnp.float32,
+                ).astype(jnp.bfloat16)
+                level = top + jnp.log(total)
+                for digit in range(3):
+                    rounded = level.astype(jnp.bfloat16).astype(jnp.float32)
+                    stats = jnp.where(lane == head * 3 + digit, rounded, stats)
+                    level = level - rounded
+            raw[chunk, row, part * span : (part + 1) * span, wide:] = stats.astype(jnp.bfloat16)
+            return inner
+
+        lax.fori_loop(0, rows, attend_row, 0)
+
+    def query_copy(chunk):
+        return pltpu.make_async_remote_copy(
+            src_ref=states.at[chunk, 0],
+            dst_ref=queries_up.at[chunk],
+            send_sem=qsend_sem.at[chunk],
+            recv_sem=qrecv_sem.at[chunk],
+            **below,
+        )
+
+    def context_copies(chunk, sources, targets, sends, receives, device):
+        return [
+            pltpu.make_async_remote_copy(
+                src_ref=source.at[chunk],
+                dst_ref=target.at[chunk],
+                send_sem=sends.at[chunk, index],
+                recv_sem=receives.at[chunk, index],
+                **device,
+            )
+            for index, (source, target) in enumerate(zip(sources, targets))
+        ]
+
+    def up_copies(chunk):
+        return context_copies(
+            chunk, (up_from, up_stats_from), (up_into, up_stats_into), usend_sem, urecv_sem, above
+        )
+
+    def down_copies(chunk):
+        return context_copies(
+            chunk, (down_from, down_stats_from), (down_into, down_stats_into), dsend_sem, drecv_sem, below
+        )
+
+    def wait_for(refs, sems, chunk):
+        for index, ref in enumerate(refs):
+            pltpu.make_async_copy(ref.at[chunk], ref.at[chunk], sems.at[chunk, index]).wait()
+
+    def exchange(chunk, head):
+        column = pl.multiple_of((2 * head + side) * head_width, head_width)
+        there = feats.at[chunk, :, :, pl.ds(column, head_width)]
+        return pltpu.make_async_remote_copy(
+            src_ref=there,
+            dst_ref=there,
+            send_sem=csend_sem.at[chunk, head],
+            recv_sem=crecv_sem.at[chunk, head],
+            **across,
+        )
+
+    def local_stage(chunk):
+        others = states.at[chunk, :, :, pl.ds(0, span - piece), :]
+        pltpu.make_async_copy(others, others, recv_sem.at[chunk]).wait()
+        mine = states.at[chunk, :, :, pl.ds(0, piece), :]
+        pltpu.make_async_copy(mine, mine, local_sem.at[chunk]).wait()
+
+        @pl.when(has_down)
+        def _():
+            query_copy(chunk).start()
+
+        attend(chunk, 0, lambda row, lanes: states[chunk, 0, row, :, lanes], own_bias)
+
+    def moved_part(moves, source, chunk, row, target):
+        moved = jnp.dot(moves[row], source, preferred_element_type=jnp.float32)
+        target[chunk, row] = moved[:, :wide].astype(jnp.bfloat16)
+        return moved[:, wide:]
+
+    def cross_stage(chunk):
+        @pl.when(has_up)
+        def _():
+            pltpu.make_async_copy(
+                queries_up.at[chunk], queries_up.at[chunk], qrecv_sem.at[chunk]
+            ).wait()
+
+        attend(chunk, 1, lambda row, lanes: queries_up[chunk, row, :, lanes], up_bias)
+
+        @pl.when(has_up)
+        def _():
+            stats = 0.0
+            for row in range(rows):
+                stats = stats + moved_part(up_moves, raw[chunk, row], chunk, row, up_from)
+            up_stats_from[chunk] = stats.astype(jnp.bfloat16)
+            for copy in up_copies(chunk):
+                copy.start()
+
+        @pl.when(gives_down)
+        def _():
+            stats = 0.0
+            for row in range(rows):
+                stats = stats + moved_part(down_moves, raw[chunk, row, :span], chunk, row, down_from)
+            down_stats_from[chunk] = stats.astype(jnp.bfloat16)
+            for copy in down_copies(chunk):
+                copy.start()
+
+        stats = 0.0
+        for row in range(rows):
+            stats = stats + moved_part(own_moves, raw[chunk, row], chunk, row, own)
+        own_stats[chunk] = stats.astype(jnp.bfloat16)
+
+    def merge_stage(chunk):
+        @pl.when(has_down)
+        def _():
+            wait_for((up_into, up_stats_into), urecv_sem, chunk)
+
+        @pl.when(gets_down)
+        def _():
+            wait_for((down_into, down_stats_into), drecv_sem, chunk)
+
+        for row in range(rows):
+            parts = (own, up_into, down_into)
+            stats = [
+                ref[chunk].astype(jnp.float32)[:, row * 8 : row * 8 + 8]
+                for ref in (own_stats, up_stats_into, down_stats_into)
+            ]
+            for head in range(2):
+                lanes = slice(head * head_width, (head + 1) * head_width)
+                levels = []
+                for stat in stats:
+                    level = stat[:, head * 3 : head * 3 + 1] + stat[:, head * 3 + 1 : head * 3 + 2]
+                    level = level + stat[:, head * 3 + 2 : head * 3 + 3]
+                    levels.append(jnp.where(stat[:, 6:7] > 0.5, level, jnp.float32(-3e30)))
+                top = jnp.maximum(jnp.maximum(levels[0], levels[1]), levels[2])
+                shares = [jnp.exp(level - top) for level in levels]
+                norm = 1.0 / (shares[0] + shares[1] + shares[2])
+                value = 0.0
+                for part, share in zip(parts, shares):
+                    value = value + part[chunk, row, :, lanes].astype(jnp.float32) * (share * norm)
+                value = value.astype(jnp.bfloat16)
+                column = pl.multiple_of((2 * head + side) * head_width, head_width)
+                for owner in range(members):
+                    feats[chunk, owner, row * piece : (row + 1) * piece, pl.ds(column, head_width)] = value[
+                        owner * piece : (owner + 1) * piece
+                    ]
+        for head in range(2):
+            exchange(chunk, head).start()
+
+    def stage(step, carry):
+        @pl.when(step < chunks)
+        def _():
+            local_stage(step)
+
+        @pl.when(jnp.logical_and(step >= 1, step <= chunks))
+        def _():
+            cross_stage(step - 1)
+
+        @pl.when(step >= 2)
+        def _():
+            merge_stage(step - 2)
+
+        for late in range(1, planes - 1):
+
+            @pl.when(step == 2 * late)
+            def _():
+                relay_weights(late)
+
+        return carry
+
+    lax.fori_loop(0, chunks + 2, stage, 0)
+
+    own_weights.wait()
+
+    def arrive(chunk, carry):
+        for head in range(2):
+            column = pl.multiple_of((2 * head + 1 - side) * head_width, head_width)
+            there = feats.at[chunk, :, :, pl.ds(column, head_width)]
+            pltpu.make_async_copy(there, there, crecv_sem.at[chunk, head]).wait()
+        return carry
+
+    lax.fori_loop(0, chunks, arrive, 0)
+
+    low_half = plane < planes // 2
+    last = jnp.where(low_half, chunks - 1, 0)
+
+    def join_early(owner, carry):
+        total = 0.0
+        for step in range(chunks - 1):
+            chunk = jnp.where(low_half, step, chunks - 1 - step)
+            total = total + jnp.dot(
+                feats[chunk, owner], weights[chunk], preferred_element_type=jnp.float32
+            )
+        sums[owner] = total
+        return carry
+
+    lax.fori_loop(0, members, join_early, 0)
+    relay_weights(planes - 1)
+
+    def partial_copy(owner):
+        return pltpu.make_async_remote_copy(
+            src_ref=partials.at[owner],
+            dst_ref=arrived.at[member],
+            send_sem=psend_sem,
+            recv_sem=precv_sem,
+            **at(plane * members + owner),
+        )
+
+    def join_last(step, carry):
+        owner = lax.rem(member + 1 + step, members)
+        total = sums[owner] + jnp.dot(
+            feats[last, owner], weights[last], preferred_element_type=jnp.float32
+        )
+        partials[owner] = total.astype(jnp.bfloat16)
+
+        @pl.when(step < members - 1)
+        def _():
+            partial_copy(owner).start()
+
+        return carry
+
+    lax.fori_loop(0, members, join_last, 0)
+    arrived[member] = partials[member]
+    incoming = arrived.at[pl.ds(0, members - 1)]
+    pltpu.make_async_copy(incoming, incoming, precv_sem).wait()
+    columns = out_ref.shape[2]
+    for row in range(rows):
+        total = 0.0
+        for source in range(members):
+            total = total + arrived[source, row * piece : (row + 1) * piece, :].astype(jnp.float32)
+        gate, up = total[:, :columns], total[:, columns:]
+        out_ref[row] = (gate / (1.0 + jnp.exp(-gate)) * up).astype(jnp.bfloat16)
+
+    def finish(chunk, carry):
+        others = states.at[chunk, :, :, pl.ds(0, span - piece), :]
+        pltpu.make_async_copy(others, others, send_sem.at[chunk]).wait()
+        for head in range(2):
+            exchange(chunk, head).wait_send()
+
+        @pl.when(has_up)
+        def _():
+            for copy in up_copies(chunk):
+                copy.wait_send()
+
+        @pl.when(has_down)
+        def _():
+            query_copy(chunk).wait_send()
+
+        @pl.when(gives_down)
+        def _():
+            for copy in down_copies(chunk):
+                copy.wait_send()
+
+        return carry
+
+    lax.fori_loop(0, chunks, finish, 0)
+    for step in range(planes):
+
+        @pl.when(jnp.logical_and(has_up, plane - step >= 0))
+        def _():
+            weight_copy(plane - step, weights.at[plane - step], 0, above).wait_send()
+
+        @pl.when(jnp.logical_and(has_down, plane + step < planes))
+        def _():
+            weight_copy(plane + step, weights.at[plane + step], 1, below).wait_send()
+
+    pltpu.make_async_copy(incoming, incoming, psend_sem).wait()
+
+
+def fused_body(queries, key_states, value_vectors, hypothesis_lengths, join_weight):
+    rows, piece, width = (queries.shape[1], queries.shape[2], queries.shape[3])
+    devices = lax.axis_size("seq")
+    planes, members = devices // PACKED_ROWS, PACKED_ROWS
+    head_width = width // ATTENTION_HEADS
+    wide = 2 * head_width
+    chunks = width // (members * wide)
+    span = members * piece
+    row_len = devices * piece
+    weight_rows, _, columns = join_weight.shape
+    first, mirror = jax.vmap(lambda lengths: hypothesis_tables(lengths, row_len))(hypothesis_lengths)
+    places = jnp.broadcast_to(jnp.arange(row_len, dtype=jnp.int32), first.shape)
+    leading = lax.axis_index("dir") == 0
+    base = lax.axis_index("seq") // members * span
+
+    def part(values, shift, absent):
+        padded = jnp.pad(values, ((0, 0), (span, span)), constant_values=absent)
+        return lax.dynamic_slice_in_dim(padded, base + span + shift, span, 1) - base
+
+    far = 4 * row_len
+    source = jnp.where(leading, places, mirror)
+    table = jnp.stack(
+        [
+            part(first, 0, far),
+            part(first, span, far),
+            part(source, 0, far),
+            part(jnp.where(leading, places, mirror), span, far),
+            part(jnp.where(leading, far, mirror), -span, far),
+        ]
+        + [jnp.zeros((rows, span), jnp.int32)] * 3,
+        axis=2,
+    )
+    geometry = (planes, rows, members, piece, head_width, chunks)
+
+    def vmem(*shape):
+        return pltpu.VMEM(shape, jnp.bfloat16)
+
+    dma = pltpu.SemaphoreType.DMA
+    context = (chunks, rows, span, wide)
+    stats = (chunks, span, head_width)
+    return pl.pallas_call(
+        functools.partial(pair_kernel, geometry),
+        out_shape=jax.ShapeDtypeStruct((rows, piece, columns), jnp.bfloat16),
+        in_specs=[pl.BlockSpec(memory_space=pltpu.VMEM)] + [pl.BlockSpec(memory_space=pl.ANY)] * 4,
+        out_specs=pl.BlockSpec(memory_space=pltpu.VMEM),
+        scratch_shapes=[
+            vmem(chunks, 3, rows, span, wide),
+            vmem(*context),
+            vmem(chunks, rows, 2 * span, wide + head_width),
+            *[vmem(*context)] * 5,
+            *[vmem(*stats)] * 5,
+            vmem(planes, weight_rows, 2 * columns),
+            vmem(chunks, members, rows * piece, 2 * wide),
+            pltpu.VMEM((members, rows * piece, 2 * columns), jnp.float32),
+            vmem(members, rows * piece, 2 * columns),
+            vmem(members, rows * piece, 2 * columns),
+            vmem(rows, span, 2 * span),
+            vmem(rows, span, 2 * span),
+            vmem(rows, span, span),
+            pltpu.VMEM((rows, span, span), jnp.float32),
+            pltpu.VMEM((rows, span, span), jnp.float32),
+            dma((chunks,)),
+            dma((chunks,)),
+            dma((chunks,)),
+            dma((chunks,)),
+            dma((chunks,)),
+            dma((chunks, 2)),
+            dma((chunks, 2)),
+            dma((chunks, 2)),
+            dma((chunks, 2)),
+            dma((2, planes)),
+            dma((planes,)),
+            dma,
+            dma((chunks, 2)),
+            dma((chunks, 2)),
+            dma,
+            dma,
+        ],
+        compiler_params=pltpu.CompilerParams(
+            collective_id=0, has_side_effects=True, vmem_limit_bytes=60 * 1024 * 1024
+        ),
+    )(
+        table,
+        queries,
+        key_states,
+        value_vectors,
+        join_weight.reshape(weight_rows, 2 * columns),
+    )
+
+
+def fits_kernel(mesh):
+    planes = mesh.shape["seq"] // PACKED_ROWS
+    return ATTENTION_HEADS // planes == 2 * PACKED_ROWS
+
+
 def solution(mesh):
     return jax.shard_map(
-        body,
+        fused_body if fits_kernel(mesh) else body,
         mesh=mesh,
         in_specs=(
             P("dir", None, "seq", None),

time: 327 us -> 185 us (0.57)
  the two profiles are of different devices: /device:TPU:0 before, /device:TPU:26 now
where the time goes in v2:
time: 185 us
  Pallas kernels  174 us (94%)
  local copies, waits for them, and re-layouts  8.84 us (5%)
  other arithmetic  2.1 us (1%)
    pallas_call x1, Pallas kernels, fused_body(): pl.pallas_call(functools.partial(pair_kernel, geometry), out_shape=jax.Sh...  174 us
    another operation x8, local copies, waits for them, and re-layouts, fused_body(): jnp.stack([part(first, 0, far), part(first, span, far), part(source, 0, f...  4.71 us
    unnamed x2, local copies, waits for them, and re-layouts  4.13 us

profile of v2, /device:TPU:26, one launch (start us, length us, event | category | flops | bytes accessed | tf_op | source)
XLA Modules:
  0.0 185.0 jit_solution(9707679685641249124)
XLA Ops:
  0.0 0.9 reduce_window_sum.11
  0.9 0.7 sub.41
  1.6 0.4 select_reduce_fusion
  2.1 0.2 copy.38
  2.4 0.2 copy.40
  2.6 0.2 copy.37
  2.8 0.2 copy.41
  3.1 0.2 copy.39
  3.3 0.8 stack.26
  4.2 2.7 %stack.27.table_ref = s32[4,256,8]{2,1,0:T(8,128)} concatenate(s32[4,256,1]{2,1,0:T(8,128)S(1)} %copy.37, s32[4,256,1]{2,1,0:T(8,128)S(1)} %copy.38, s32[4,256,1]{2,1,0:T(8,128)S(1)} %copy.39, s32[4,256,1]{2,1,0:T(8,128)S(1)} %copy.40, s32[4,256,1]{2,1,0:T(8,128)S(1)} %copy.41, s32[4,256,1]{2,1,0:T(8,128)S(1)} %stack_broadcast_in_dim.3, s32[4,256,2]{2,1,0:T(8,128)} %stack.26), dimensions={2} | concatenate | bytes 65536 | tf_op jit(solution)/shard_map/stack | solution.py:561
  6.9 2.5 %copy.42 = bf16[64,8,2,512]{3,1,2,0:T(8,128)(2,1)} copy(bf16[64,8,2,512]{3,2,1,0:T(2,128)(2,1)} %bitcast.13) | data formatting | bytes 2097152
  9.3 174.0 %shard_map.55 = bf16[4,64,512]{2,1,0:T(8,128)(2,1)} custom-call(s32[4,256,8]{2,1,0:T(8,128)} %stack.27.table_ref, bf16[1,4,64,4096]{3,2,1,0:T(8,128)(2,1)} %q_ref.1, bf16[1,4,64,4096]{3,2,1,0:T(8,128)(2,1)} %k_ref.1, bf16[1,4,64,4096]{3,2,1,0:T(8,128)(2,1)} %v_ref.1, bf16[512,1024]{1,0:T(8,128)(2,1)} %bitcast.12), custom_call_target="tpu_custom_call" | custom-call | tf_op jit(solution)/shard_map/pallas_call | solution.py:580
  183.4 1.7 copy.44
  (4 shorter events, 0.1 us)

commit v3 on v2

--- a/solution.py
+++ b/solution.py
@@ -118,14 +118,14 @@
 
 
 def pair_kernel(
-    geometry, table_ref, q_ref, k_ref, v_ref, weight_ref, out_ref,
+    geometry, lengths_ref, q_ref, k_ref, v_ref, weight_ref, out_ref,
     states, queries_up, raw, own, up_from, up_into, down_from, down_into,
     own_stats, up_stats_from, up_stats_into, down_stats_from, down_stats_into,
     weights, feats, sums, partials, arrived, own_moves, up_moves, down_moves, own_bias, up_bias,
     send_sem, recv_sem, local_sem, qsend_sem, qrecv_sem, usend_sem, urecv_sem, dsend_sem, drecv_sem,
     wsend_sem, wrecv_sem, wlocal_sem, csend_sem, crecv_sem, psend_sem, precv_sem,
 ):
-    planes, rows, members, piece, head_width, chunks = geometry
+    planes, rows, members, piece, head_width, chunks, halves = geometry
     side = lax.axis_index("dir")
     me = lax.axis_index("seq")
     plane, member = lax.div(me, members), lax.rem(me, members)
@@ -158,12 +158,12 @@
 
     pl.semaphore_wait(barrier, members + jnp.where(has_up, 1, 0) + jnp.where(has_down, 1, 0))
 
-    def weight_copy(shard, source, way, target):
+    def weight_copy(shard, half, source, way, target):
         return pltpu.make_async_remote_copy(
             src_ref=source,
-            dst_ref=weights.at[shard],
-            send_sem=wsend_sem.at[way, shard],
-            recv_sem=wrecv_sem.at[shard],
+            dst_ref=weights.at[shard, half],
+            send_sem=wsend_sem.at[way, shard, half],
+            recv_sem=wrecv_sem.at[shard, half],
             **target,
         )
 
@@ -194,33 +194,35 @@
 
     @pl.when(has_up)
     def _():
-        weight_copy(plane, weight_ref, 0, above).start()
+        for half in range(halves):
+            weight_copy(plane, half, weight_ref.at[half], 0, above).start()
 
     @pl.when(has_down)
     def _():
-        weight_copy(plane, weight_ref, 1, below).start()
+        for half in range(halves):
+            weight_copy(plane, half, weight_ref.at[half], 1, below).start()
 
     own_weights = pltpu.make_async_copy(weight_ref, weights.at[plane], wlocal_sem)
     own_weights.start()
 
-    def relay_weights(step):
+    def relay_weights(step, half):
         @pl.when(plane - step >= 0)
         def _():
-            shard = weights.at[plane - step]
-            pltpu.make_async_copy(shard, shard, wrecv_sem.at[plane - step]).wait()
+            shard = weights.at[plane - step, half]
+            pltpu.make_async_copy(shard, shard, wrecv_sem.at[plane - step, half]).wait()
 
             @pl.when(has_up)
             def _():
-                weight_copy(plane - step, shard, 0, above).start()
+                weight_copy(plane - step, half, shard, 0, above).start()
 
         @pl.when(plane + step < planes)
         def _():
-            shard = weights.at[plane + step]
-            pltpu.make_async_copy(shard, shard, wrecv_sem.at[plane + step]).wait()
+            shard = weights.at[plane + step, half]
+            pltpu.make_async_copy(shard, shard, wrecv_sem.at[plane + step, half]).wait()
 
             @pl.when(has_down)
             def _():
-                weight_copy(plane + step, shard, 1, below).start()
+                weight_copy(plane + step, half, shard, 1, below).start()
 
     @pl.when(jnp.logical_not(has_up))
     def _():
@@ -239,20 +241,45 @@
         down_into[...] = jnp.zeros_like(down_into)
         down_stats_into[...] = jnp.zeros_like(down_stats_into)
 
-    def tables(row, carry):
-        table = table_ref[row]
-        k_places = lax.broadcasted_iota(jnp.int32, (span, span), 1)
-        q_places = lax.broadcasted_iota(jnp.int32, (span, span), 0)
-        places = lax.broadcasted_iota(jnp.int32, (span, 2 * span), 1)
-        allowed = (k_places >= table[:, 0:1]) & (k_places <= q_places)
+    slots = lengths_ref.shape[1]
+    before = lax.broadcasted_iota(jnp.int32, (slots, slots), 0)
+    after = lax.broadcasted_iota(jnp.int32, (slots, slots), 1)
+    lengths = lengths_ref[...].astype(jnp.float32)
+    all_ends = jnp.dot(
+        lengths.astype(jnp.bfloat16),
+        jnp.where(before <= after, 1.0, 0.0).astype(jnp.bfloat16),
+        preferred_element_type=jnp.float32,
+    )
+    base = plane * span
+    far = 4 * planes * span
+
+    def places_of(row, shift):
+        ends = all_ends[row : row + 1].astype(jnp.int32)
+        starts = ends - lengths_ref[row : row + 1]
+        wide_places = base + shift + lax.broadcasted_iota(jnp.int32, (span, slots), 0)
+        inside = (wide_places >= starts) & (wide_places < ends)
+        place = base + shift + lax.broadcasted_iota(jnp.int32, (span, 1), 0)
+        first = jnp.sum(jnp.where(inside, starts, 0), axis=1, keepdims=True)
+        last = jnp.sum(jnp.where(inside, ends, 0), axis=1, keepdims=True) - 1
+        return first - base, place - base, first + last - place - base
+
+    k_places = lax.broadcasted_iota(jnp.int32, (span, span), 1)
+    q_places = lax.broadcasted_iota(jnp.int32, (span, span), 0)
+    places = lax.broadcasted_iota(jnp.int32, (span, 2 * span), 1)
+    for row in range(rows):
+        first, place, mirror = places_of(row, 0)
+        allowed = (k_places >= first) & (k_places <= q_places)
         own_bias[row] = jnp.where(allowed, jnp.float32(0), jnp.float32(-1e30))
-        up_bias[row] = jnp.where(k_places >= table[:, 1:2], jnp.float32(0), jnp.float32(-1e30))
-        own_moves[row] = jnp.where(places == table[:, 2:3], 1.0, 0.0).astype(jnp.bfloat16)
-        up_moves[row] = jnp.where(places == table[:, 3:4], 1.0, 0.0).astype(jnp.bfloat16)
-        down_moves[row] = jnp.where(k_places == table[:, 4:5], 1.0, 0.0).astype(jnp.bfloat16)
-        return carry
-
-    lax.fori_loop(0, rows, tables, 0)
+        source = jnp.where(side == 0, place, mirror)
+        own_moves[row] = jnp.where(places == source, 1.0, 0.0).astype(jnp.bfloat16)
+        first, place, mirror = places_of(row, span)
+        first = jnp.where(has_up, first, far)
+        up_bias[row] = jnp.where(k_places >= first, jnp.float32(0), jnp.float32(-1e30))
+        source = jnp.where(side == 0, place, mirror)
+        up_moves[row] = jnp.where(places == source, 1.0, 0.0).astype(jnp.bfloat16)
+        first, place, mirror = places_of(row, -span)
+        source = jnp.where(gives_down, mirror, far)
+        down_moves[row] = jnp.where(k_places == source, 1.0, 0.0).astype(jnp.bfloat16)
 
     def attend(chunk, part, q_of, bias_ref):
         def attend_row(row, inner):
@@ -422,6 +449,13 @@
         def _():
             local_stage(step)
 
+        for late in range(1, planes - 1):
+
+            @pl.when(step == late)
+            def _():
+                for half in range(halves):
+                    relay_weights(late, half)
+
         @pl.when(jnp.logical_and(step >= 1, step <= chunks))
         def _():
             cross_stage(step - 1)
@@ -429,12 +463,6 @@
         @pl.when(step >= 2)
         def _():
             merge_stage(step - 2)
-
-        for late in range(1, planes - 1):
-
-            @pl.when(step == 2 * late)
-            def _():
-                relay_weights(late)
 
         return carry
 
@@ -455,51 +483,62 @@
     last = jnp.where(low_half, chunks - 1, 0)
 
     def join_early(owner, carry):
-        total = 0.0
-        for step in range(chunks - 1):
-            chunk = jnp.where(low_half, step, chunks - 1 - step)
-            total = total + jnp.dot(
-                feats[chunk, owner], weights[chunk], preferred_element_type=jnp.float32
+        for half in range(halves):
+            total = 0.0
+            for step in range(chunks - 1):
+                chunk = jnp.where(low_half, step, chunks - 1 - step)
+                total = total + jnp.dot(
+                    feats[chunk, owner], weights[chunk, half], preferred_element_type=jnp.float32
+                )
+            sums[half, owner] = total
+        return carry
+
+    lax.fori_loop(0, members, join_early, 0)
+
+    def partial_copy(half, owner):
+        return pltpu.make_async_remote_copy(
+            src_ref=partials.at[half, owner],
+            dst_ref=arrived.at[half, member],
+            send_sem=psend_sem.at[half],
+            recv_sem=precv_sem.at[half],
+            **at(plane * members + owner),
+        )
+
+    def join_half(half, carry):
+        relay_weights(planes - 1, half)
+
+        def join_last(step, inner):
+            owner = lax.rem(member + 1 + step, members)
+            total = sums[half, owner] + jnp.dot(
+                feats[last, owner], weights[last, half], preferred_element_type=jnp.float32
             )
-        sums[owner] = total
+            partials[half, owner] = total.astype(jnp.bfloat16)
+
+            @pl.when(step < members - 1)
+            def _():
+                partial_copy(half, owner).start()
+
+            return inner
+
+        lax.fori_loop(0, members, join_last, 0)
+        arrived[half, member] = partials[half, member]
         return carry
 
-    lax.fori_loop(0, members, join_early, 0)
-    relay_weights(planes - 1)
-
-    def partial_copy(owner):
-        return pltpu.make_async_remote_copy(
-            src_ref=partials.at[owner],
-            dst_ref=arrived.at[member],
-            send_sem=psend_sem,
-            recv_sem=precv_sem,
-            **at(plane * members + owner),
-        )
-
-    def join_last(step, carry):
-        owner = lax.rem(member + 1 + step, members)
-        total = sums[owner] + jnp.dot(
-            feats[last, owner], weights[last], preferred_element_type=jnp.float32
-        )
-        partials[owner] = total.astype(jnp.bfloat16)
-
-        @pl.when(step < members - 1)
-        def _():
-            partial_copy(owner).start()
-
-        return carry
-
-    lax.fori_loop(0, members, join_last, 0)
-    arrived[member] = partials[member]
-    incoming = arrived.at[pl.ds(0, members - 1)]
-    pltpu.make_async_copy(incoming, incoming, precv_sem).wait()
-    columns = out_ref.shape[2]
-    for row in range(rows):
-        total = 0.0
-        for source in range(members):
-            total = total + arrived[source, row * piece : (row + 1) * piece, :].astype(jnp.float32)
-        gate, up = total[:, :columns], total[:, columns:]
-        out_ref[row] = (gate / (1.0 + jnp.exp(-gate)) * up).astype(jnp.bfloat16)
+    lax.fori_loop(0, halves, join_half, 0)
+    columns = out_ref.shape[2] // halves
+    for half in range(halves):
+        incoming = arrived.at[half, pl.ds(0, members - 1)]
+        pltpu.make_async_copy(incoming, incoming, precv_sem.at[half]).wait()
+        for row in range(rows):
+            total = 0.0
+            for source in range(members):
+                total = total + arrived[half, source, row * piece : (row + 1) * piece, :].astype(
+                    jnp.float32
+                )
+            gate, up = total[:, :columns], total[:, columns:]
+            out_ref[row, :, half * columns : (half + 1) * columns] = (
+                gate / (1.0 + jnp.exp(-gate)) * up
+            ).astype(jnp.bfloat16)
 
     def finish(chunk, carry):
         others = states.at[chunk, :, :, pl.ds(0, span - piece), :]
@@ -528,13 +567,17 @@
 
         @pl.when(jnp.logical_and(has_up, plane - step >= 0))
         def _():
-            weight_copy(plane - step, weights.at[plane - step], 0, above).wait_send()
+            for half in range(halves):
+                weight_copy(plane - step, half, weights.at[plane - step, half], 0, above).wait_send()
 
         @pl.when(jnp.logical_and(has_down, plane + step < planes))
         def _():
-            weight_copy(plane + step, weights.at[plane + step], 1, below).wait_send()
-
-    pltpu.make_async_copy(incoming, incoming, psend_sem).wait()
+            for half in range(halves):
+                weight_copy(plane + step, half, weights.at[plane + step, half], 1, below).wait_send()
+
+    for half in range(halves):
+        incoming = arrived.at[half, pl.ds(0, members - 1)]
+        pltpu.make_async_copy(incoming, incoming, psend_sem.at[half]).wait()
 
 
 def fused_body(queries, key_states, value_vectors, hypothesis_lengths, join_weight):
@@ -545,31 +588,11 @@
     wide = 2 * head_width
     chunks = width // (members * wide)
     span = members * piece
-    row_len = devices * piece
+    halves = 2
     weight_rows, _, columns = join_weight.shape
-    first, mirror = jax.vmap(lambda lengths: hypothesis_tables(lengths, row_len))(hypothesis_lengths)
-    places = jnp.broadcast_to(jnp.arange(row_len, dtype=jnp.int32), first.shape)
-    leading = lax.axis_index("dir") == 0
-    base = lax.axis_index("seq") // members * span
-
-    def part(values, shift, absent):
-        padded = jnp.pad(values, ((0, 0), (span, span)), constant_values=absent)
-        return lax.dynamic_slice_in_dim(padded, base + span + shift, span, 1) - base
-
-    far = 4 * row_len
-    source = jnp.where(leading, places, mirror)
-    table = jnp.stack(
-        [
-            part(first, 0, far),
-            part(first, span, far),
-            part(source, 0, far),
-            part(jnp.where(leading, places, mirror), span, far),
-            part(jnp.where(leading, far, mirror), -span, far),
-        ]
-        + [jnp.zeros((rows, span), jnp.int32)] * 3,
-        axis=2,
-    )
-    geometry = (planes, rows, members, piece, head_width, chunks)
+    part = columns // halves
+    by_halves = jnp.transpose(join_weight.reshape(weight_rows, 2, halves, part), (2, 0, 1, 3))
+    geometry = (planes, rows, members, piece, head_width, chunks, halves)
 
     def vmem(*shape):
         return pltpu.VMEM(shape, jnp.bfloat16)
@@ -588,11 +611,11 @@
             vmem(chunks, rows, 2 * span, wide + head_width),
             *[vmem(*context)] * 5,
             *[vmem(*stats)] * 5,
-            vmem(planes, weight_rows, 2 * columns),
+            vmem(planes, halves, weight_rows, 2 * part),
             vmem(chunks, members, rows * piece, 2 * wide),
-            pltpu.VMEM((members, rows * piece, 2 * columns), jnp.float32),
-            vmem(members, rows * piece, 2 * columns),
-            vmem(members, rows * piece, 2 * columns),
+            pltpu.VMEM((halves, members, rows * piece, 2 * part), jnp.float32),
+            vmem(halves, members, rows * piece, 2 * part),
+            vmem(halves, members, rows * piece, 2 * part),
             vmem(rows, span, 2 * span),
             vmem(rows, span, 2 * span),
             vmem(rows, span, span),
@@ -607,23 +630,23 @@
             dma((chunks, 2)),
             dma((chunks, 2)),
             dma((chunks, 2)),
-            dma((2, planes)),
-            dma((planes,)),
+            dma((2, planes, halves)),
+            dma((planes, halves)),
             dma,
             dma((chunks, 2)),
             dma((chunks, 2)),
-            dma,
-            dma,
+            dma((halves,)),
+            dma((halves,)),
         ],
         compiler_params=pltpu.CompilerParams(
             collective_id=0, has_side_effects=True, vmem_limit_bytes=60 * 1024 * 1024
         ),
     )(
-        table,
+        hypothesis_lengths,
         queries,
         key_states,
         value_vectors,
-        join_weight.reshape(weight_rows, 2 * columns),
+        by_halves.reshape(halves, weight_rows, 2 * part),
     )
 
 

time: 185 us -> 185 us (level)
  the two profiles are of different devices: /device:TPU:26 before, /device:TPU:0 now
where the time goes in v3:
time: 185 us
  Pallas kernels  180 us (97%)
  local copies, waits for them, and re-layouts  5.12 us (3%)
    pallas_call x1, Pallas kernels, fused_body(): pl.pallas_call(functools.partial(pair_kernel, geometry), out_shape=jax.Sh...  180 us

profile of v3, /device:TPU:0, one launch (start us, length us, event | category | flops | bytes accessed | tf_op | source)
XLA Modules:
  0.0 185.1 jit_solution(15364143089667396214)
XLA Ops:
  0.0 1.9 %copy.9 = bf16[512,1,2,2,256]{4,3,1,0,2:T(2,128)(2,1)S(1)} copy(bf16[512,1,2,2,256]{4,3,2,1,0:T(2,128)(2,1)} %bitcast.8) | data formatting | bytes 2097152 | tf_op jit(solution)/shard_map/reshape | solution.py:594
  1.9 1.5 reshape.7.weight_ref
  3.5 180.0 %shard_map.55 = bf16[4,64,512]{2,1,0:T(8,128)(2,1)} custom-call(s32[4,64]{1,0:T(4,128)} %lengths_ref.1, bf16[1,4,64,4096]{3,2,1,0:T(8,128)(2,1)} %q_ref.1, bf16[1,4,64,4096]{3,2,1,0:T(8,128)(2,1)} %k_ref.1, bf16[1,4,64,4096]{3,2,1,0:T(8,128)(2,1)} %v_ref.1, bf16[2,512,512]{2,1,0:T(8,128)(2,1)} %reshape.7.weight_ref), custom_call_target="tpu_custom_call" | custom-call | tf_op jit(solution)/shard_map/pallas_call | solution.py:603
  183.4 1.7 copy.11

commit v4 on v3

--- a/solution.py
+++ b/solution.py
@@ -173,7 +173,7 @@
     def landing(chunk, index):
         return states.at[chunk, index, :, pl.ds(pl.multiple_of(member * piece, piece), piece), :]
 
-    def send_chunk(chunk, carry):
+    def send_chunk(chunk):
         for step in range(1, members):
             owner = lax.rem(member + step, members)
             for index, ref in enumerate((q_ref, k_ref, v_ref)):
@@ -188,19 +188,22 @@
             pltpu.make_async_copy(
                 ref.at[0, :, :, input_column(chunk, member)], landing(chunk, index), local_sem.at[chunk]
             ).start()
+
+    def send_own_weights(half):
+        @pl.when(has_up)
+        def _():
+            weight_copy(plane, half, weight_ref.at[half], 0, above).start()
+
+        @pl.when(has_down)
+        def _():
+            weight_copy(plane, half, weight_ref.at[half], 1, below).start()
+
+    def send_first(chunk, carry):
+        send_chunk(chunk)
+        send_own_weights(chunk)
         return carry
 
-    lax.fori_loop(0, chunks, send_chunk, 0)
-
-    @pl.when(has_up)
-    def _():
-        for half in range(halves):
-            weight_copy(plane, half, weight_ref.at[half], 0, above).start()
-
-    @pl.when(has_down)
-    def _():
-        for half in range(halves):
-            weight_copy(plane, half, weight_ref.at[half], 1, below).start()
+    lax.fori_loop(0, halves, send_first, 0)
 
     own_weights = pltpu.make_async_copy(weight_ref, weights.at[plane], wlocal_sem)
     own_weights.start()
@@ -367,6 +370,10 @@
         @pl.when(has_down)
         def _():
             query_copy(chunk).start()
+
+        @pl.when(chunk + halves < chunks)
+        def _():
+            send_chunk(chunk + halves)
 
         attend(chunk, 0, lambda row, lanes: states[chunk, 0, row, :, lanes], own_bias)
 

time: 185 us -> 185 us (level)
  no operation moved by 1% of the time
where the time goes in v4:
time: 185 us
  Pallas kernels  180 us (97%)
  local copies, waits for them, and re-layouts  5.12 us (3%)
    pallas_call x1, Pallas kernels, fused_body(): pl.pallas_call(functools.partial(pair_kernel, geometry), out_shape=jax.Sh...  180 us

profile of v4, /device:TPU:0, one launch (start us, length us, event | category | flops | bytes accessed | tf_op | source)
XLA Modules:
  0.0 185.1 jit_solution(2294080380622740707)
XLA Ops:
  0.0 1.9 %copy.9 = bf16[512,1,2,2,256]{4,3,1,0,2:T(2,128)(2,1)S(1)} copy(bf16[512,1,2,2,256]{4,3,2,1,0:T(2,128)(2,1)} %bitcast.8) | data formatting | bytes 2097152 | tf_op jit(solution)/shard_map/reshape | solution.py:601
  1.9 1.5 reshape.7.weight_ref
  3.5 180.0 %shard_map.55 = bf16[4,64,512]{2,1,0:T(8,128)(2,1)} custom-call(s32[4,64]{1,0:T(4,128)} %lengths_ref.1, bf16[1,4,64,4096]{3,2,1,0:T(8,128)(2,1)} %q_ref.1, bf16[1,4,64,4096]{3,2,1,0:T(8,128)(2,1)} %k_ref.1, bf16[1,4,64,4096]{3,2,1,0:T(8,128)(2,1)} %v_ref.1, bf16[2,512,512]{2,1,0:T(8,128)(2,1)} %reshape.7.weight_ref), custom_call_target="tpu_custom_call" | custom-call | tf_op jit(solution)/shard_map/pallas_call | solution.py:610
  183.4 1.7 copy.11

commit v5 on v4

--- a/solution.py
+++ b/solution.py
@@ -285,32 +285,47 @@
         down_moves[row] = jnp.where(k_places == source, 1.0, 0.0).astype(jnp.bfloat16)
 
     def attend(chunk, part, q_of, bias_ref):
+        reach = span // 2
+
         def attend_row(row, inner):
-            lane = lax.broadcasted_iota(jnp.int32, (span, head_width), 1) - row * 8
-            stats = jnp.where(lane == 6, jnp.float32(1), jnp.float32(0))
-            for head in range(2):
-                lanes = slice(head * head_width, (head + 1) * head_width)
-                scores = lax.dot_general(
-                    q_of(row, lanes),
-                    states[chunk, 1, row, :, lanes],
-                    (((1,), (1,)), ((), ())),
-                    preferred_element_type=jnp.float32,
+            lane = lax.broadcasted_iota(jnp.int32, (reach, head_width), 1) - row * 8
+            mine = (lane >= 0) & (lane < 6)
+            for half in range(2):
+                at_rows = slice(half * reach, (half + 1) * reach)
+                keys = slice(0, (half + 1) * reach) if part == 0 else slice(half * reach, span)
+                placed = slice(part * span + half * reach, part * span + (half + 1) * reach)
+                tops, totals = [], []
+                for head in range(2):
+                    lanes = slice(head * head_width, (head + 1) * head_width)
+                    scores = lax.dot_general(
+                        q_of(row, at_rows, lanes),
+                        states[chunk, 1, row, keys, lanes],
+                        (((1,), (1,)), ((), ())),
+                        preferred_element_type=jnp.float32,
+                    )
+                    scores = scores * scale + bias_ref[row, at_rows, keys]
+                    top = jnp.max(scores, axis=1, keepdims=True)
+                    raised = jnp.exp(scores - top)
+                    total = jnp.sum(raised, axis=1, keepdims=True)
+                    raw[chunk, row, placed, lanes] = jnp.dot(
+                        (raised * (1.0 / total)).astype(jnp.bfloat16),
+                        states[chunk, 2, row, keys, lanes],
+                        preferred_element_type=jnp.float32,
+                    ).astype(jnp.bfloat16)
+                    tops.append(top)
+                    totals.append(total)
+                level = jnp.where(lane >= 3, tops[1], tops[0]) + jnp.log(
+                    jnp.where(lane >= 3, totals[1], totals[0])
                 )
-                scores = scores * scale + bias_ref[row]
-                top = jnp.max(scores, axis=1, keepdims=True)
-                raised = jnp.exp(scores - top)
-                total = jnp.sum(raised, axis=1, keepdims=True)
-                raw[chunk, row, part * span : (part + 1) * span, lanes] = jnp.dot(
-                    (raised * (1.0 / total)).astype(jnp.bfloat16),
-                    states[chunk, 2, row, :, lanes],
-                    preferred_element_type=jnp.float32,
-                ).astype(jnp.bfloat16)
-                level = top + jnp.log(total)
-                for digit in range(3):
-                    rounded = level.astype(jnp.bfloat16).astype(jnp.float32)
-                    stats = jnp.where(lane == head * 3 + digit, rounded, stats)
-                    level = level - rounded
-            raw[chunk, row, part * span : (part + 1) * span, wide:] = stats.astype(jnp.bfloat16)
+                high = level.astype(jnp.bfloat16).astype(jnp.float32)
+                level = level - high
+                middle = level.astype(jnp.bfloat16).astype(jnp.float32)
+                low = level - middle
+                digits = jnp.where(
+                    (lane == 0) | (lane == 3), high, jnp.where((lane == 1) | (lane == 4), middle, low)
+                )
+                digits = jnp.where(mine, digits, jnp.where(lane == 6, 1.0, 0.0))
+                raw[chunk, row, placed, wide:] = digits.astype(jnp.bfloat16)
             return inner
 
         lax.fori_loop(0, rows, attend_row, 0)
@@ -375,7 +390,7 @@
         def _():
             send_chunk(chunk + halves)
 
-        attend(chunk, 0, lambda row, lanes: states[chunk, 0, row, :, lanes], own_bias)
+        attend(chunk, 0, lambda row, at_rows, lanes: states[chunk, 0, row, at_rows, lanes], own_bias)
 
     def moved_part(moves, source, chunk, row, target):
         moved = jnp.dot(moves[row], source, preferred_element_type=jnp.float32)
@@ -389,7 +404,7 @@
                 queries_up.at[chunk], queries_up.at[chunk], qrecv_sem.at[chunk]
             ).wait()
 
-        attend(chunk, 1, lambda row, lanes: queries_up[chunk, row, :, lanes], up_bias)
+        attend(chunk, 1, lambda row, at_rows, lanes: queries_up[chunk, row, at_rows, lanes], up_bias)
 
         @pl.when(has_up)
         def _():
@@ -423,25 +438,30 @@
         def _():
             wait_for((down_into, down_stats_into), drecv_sem, chunk)
 
+        lane_in = lax.broadcasted_iota(jnp.int32, (head_width, head_width), 0)
+        lane_out = lax.broadcasted_iota(jnp.int32, (head_width, head_width), 1)
+        same_row = lane_in // 8 == lane_out // 8
+        digit_in, digit_out = lane_in % 8, lane_out % 8
+        same_head = (digit_in < 6) & ((digit_in >= 3) == (digit_out >= 3))
+        gather = jnp.where(same_row & same_head, 1.0, 0.0).astype(jnp.bfloat16)
+        marks = jnp.where(same_row & (digit_in == 6), 1.0, 0.0).astype(jnp.bfloat16)
+        levels = []
+        for ref in (own_stats, up_stats_into, down_stats_into):
+            stat = ref[chunk]
+            level = jnp.dot(stat, gather, preferred_element_type=jnp.float32)
+            present = jnp.dot(stat, marks, preferred_element_type=jnp.float32)
+            levels.append(jnp.where(present > 0.5, level, jnp.float32(-3e30)))
+        top = jnp.maximum(jnp.maximum(levels[0], levels[1]), levels[2])
+        shares = [jnp.exp(level - top) for level in levels]
+        norm = 1.0 / (shares[0] + shares[1] + shares[2])
+        shares = [share * norm for share in shares]
         for row in range(rows):
-            parts = (own, up_into, down_into)
-            stats = [
-                ref[chunk].astype(jnp.float32)[:, row * 8 : row * 8 + 8]
-                for ref in (own_stats, up_stats_into, down_stats_into)
-            ]
             for head in range(2):
                 lanes = slice(head * head_width, (head + 1) * head_width)
-                levels = []
-                for stat in stats:
-                    level = stat[:, head * 3 : head * 3 + 1] + stat[:, head * 3 + 1 : head * 3 + 2]
-                    level = level + stat[:, head * 3 + 2 : head * 3 + 3]
-                    levels.append(jnp.where(stat[:, 6:7] > 0.5, level, jnp.float32(-3e30)))
-                top = jnp.maximum(jnp.maximum(levels[0], levels[1]), levels[2])
-                shares = [jnp.exp(level - top) for level in levels]
-                norm = 1.0 / (shares[0] + shares[1] + shares[2])
+                lane = row * 8 + head * 3
                 value = 0.0
-                for part, share in zip(parts, shares):
-                    value = value + part[chunk, row, :, lanes].astype(jnp.float32) * (share * norm)
+                for part, share in zip((own, up_into, down_into), shares):
+                    value = value + part[chunk, row, :, lanes].astype(jnp.float32) * share[:, lane : lane + 1]
                 value = value.astype(jnp.bfloat16)
                 column = pl.multiple_of((2 * head + side) * head_width, head_width)
                 for owner in range(members):

time: 185 us -> 183 us (0.989)
  Pallas kernels: 180 us -> 178 us
    pallas_call x1, Pallas kernels: 180 us -> 178 us  [fused_body(): pl.pallas_call(functools.partial(pair_kernel, geometry), out_shape=jax.Sh...]
where the time goes in v5:
time: 183 us
  Pallas kernels  178 us (97%)
  local copies, waits for them, and re-layouts  5.12 us (3%)
    pallas_call x1, Pallas kernels, fused_body(): pl.pallas_call(functools.partial(pair_kernel, geometry), out_shape=jax.Sh...  178 us

profile of v5, /device:TPU:0, one launch (start us, length us, event | category | flops | bytes accessed | tf_op | source)
XLA Modules:
  0.0 182.8 jit_solution(4502915079741193384)
XLA Ops:
  0.0 1.9 %copy.9 = bf16[512,1,2,2,256]{4,3,1,0,2:T(2,128)(2,1)S(1)} copy(bf16[512,1,2,2,256]{4,3,2,1,0:T(2,128)(2,1)} %bitcast.8) | data formatting | bytes 2097152 | tf_op jit(solution)/shard_map/reshape | solution.py:621
  1.9 1.5 reshape.7.weight_ref
  3.5 177.7 %shard_map.55 = bf16[4,64,512]{2,1,0:T(8,128)(2,1)} custom-call(s32[4,64]{1,0:T(4,128)} %lengths_ref.1, bf16[1,4,64,4096]{3,2,1,0:T(8,128)(2,1)} %q_ref.1, bf16[1,4,64,4096]{3,2,1,0:T(8,128)(2,1)} %k_ref.1, bf16[1,4,64,4096]{3,2,1,0:T(8,128)(2,1)} %v_ref.1, bf16[2,512,512]{2,1,0:T(8,128)(2,1)} %reshape.7.weight_ref), custom_call_target="tpu_custom_call" | custom-call | tf_op jit(solution)/shard_map/pallas_call | solution.py:630
  181.1 1.7 copy.11

commit v6 on v5

--- a/solution.py
+++ b/solution.py
@@ -476,16 +476,16 @@
         def _():
             local_stage(step)
 
+        @pl.when(jnp.logical_and(step >= 1, step <= chunks))
+        def _():
+            cross_stage(step - 1)
+
         for late in range(1, planes - 1):
 
-            @pl.when(step == late)
+            @pl.when(step == 2 * late)
             def _():
                 for half in range(halves):
                     relay_weights(late, half)
-
-        @pl.when(jnp.logical_and(step >= 1, step <= chunks))
-        def _():
-            cross_stage(step - 1)
 
         @pl.when(step >= 2)
         def _():

time: 183 us -> 172 us (0.940)
  Pallas kernels: 178 us -> 167 us
    pallas_call x1, Pallas kernels: 178 us -> 167 us  [fused_body(): pl.pallas_call(functools.partial(pair_kernel, geometry), out_shape=jax.Sh...]
where the time goes in v6:
time: 172 us
  Pallas kernels  167 us (97%)
  local copies, waits for them, and re-layouts  5.12 us (3%)
    pallas_call x1, Pallas kernels, fused_body(): pl.pallas_call(functools.partial(pair_kernel, geometry), out_shape=jax.Sh...  167 us

profile of v6, /device:TPU:0, one launch (start us, length us, event | category | flops | bytes accessed | tf_op | source)
XLA Modules:
  0.0 171.8 jit_solution(751250492499122987)
XLA Ops:
  0.0 1.9 %copy.9 = bf16[512,1,2,2,256]{4,3,1,0,2:T(2,128)(2,1)S(1)} copy(bf16[512,1,2,2,256]{4,3,2,1,0:T(2,128)(2,1)} %bitcast.8) | data formatting | bytes 2097152 | tf_op jit(solution)/shard_map/reshape | solution.py:621
  1.9 1.5 reshape.7.weight_ref
  3.5 166.7 %shard_map.55 = bf16[4,64,512]{2,1,0:T(8,128)(2,1)} custom-call(s32[4,64]{1,0:T(4,128)} %lengths_ref.1, bf16[1,4,64,4096]{3,2,1,0:T(8,128)(2,1)} %q_ref.1, bf16[1,4,64,4096]{3,2,1,0:T(8,128)(2,1)} %k_ref.1, bf16[1,4,64,4096]{3,2,1,0:T(8,128)(2,1)} %v_ref.1, bf16[2,512,512]{2,1,0:T(8,128)(2,1)} %reshape.7.weight_ref), custom_call_target="tpu_custom_call" | custom-call | tf_op jit(solution)/shard_map/pallas_call | solution.py:630
  170.1 1.7 copy.11

commit v7 on v6

--- a/solution.py
+++ b/solution.py
@@ -121,7 +121,7 @@
     geometry, lengths_ref, q_ref, k_ref, v_ref, weight_ref, out_ref,
     states, queries_up, raw, own, up_from, up_into, down_from, down_into,
     own_stats, up_stats_from, up_stats_into, down_stats_from, down_stats_into,
-    weights, feats, sums, partials, arrived, own_moves, up_moves, down_moves, own_bias, up_bias,
+    weights, feats, sums, partials, arrived, own_moves, up_moves, down_moves, spread_moves, own_bias, up_bias,
     send_sem, recv_sem, local_sem, qsend_sem, qrecv_sem, usend_sem, urecv_sem, dsend_sem, drecv_sem,
     wsend_sem, wrecv_sem, wlocal_sem, csend_sem, crecv_sem, psend_sem, precv_sem,
 ):
@@ -275,14 +275,18 @@
         own_bias[row] = jnp.where(allowed, jnp.float32(0), jnp.float32(-1e30))
         source = jnp.where(side == 0, place, mirror)
         own_moves[row] = jnp.where(places == source, 1.0, 0.0).astype(jnp.bfloat16)
+        slot = lax.broadcasted_iota(jnp.int32, (span // 2, span), 0)
+        final = mirror[0:1] - first[0:1]
+        given = (slot < -first[0:1]) & (k_places[: span // 2] == final - slot)
+        down_moves[row] = jnp.where(given, 1.0, 0.0).astype(jnp.bfloat16)
+        slot = lax.broadcasted_iota(jnp.int32, (span, span // 2), 1)
+        taken = (mirror >= span) & (slot == place - first)
+        spread_moves[row] = jnp.where(taken, 1.0, 0.0).astype(jnp.bfloat16)
         first, place, mirror = places_of(row, span)
         first = jnp.where(has_up, first, far)
         up_bias[row] = jnp.where(k_places >= first, jnp.float32(0), jnp.float32(-1e30))
         source = jnp.where(side == 0, place, mirror)
         up_moves[row] = jnp.where(places == source, 1.0, 0.0).astype(jnp.bfloat16)
-        first, place, mirror = places_of(row, -span)
-        source = jnp.where(gives_down, mirror, far)
-        down_moves[row] = jnp.where(k_places == source, 1.0, 0.0).astype(jnp.bfloat16)
 
     def attend(chunk, part, q_of, bias_ref):
         reach = span // 2
@@ -445,9 +449,15 @@
         same_head = (digit_in < 6) & ((digit_in >= 3) == (digit_out >= 3))
         gather = jnp.where(same_row & same_head, 1.0, 0.0).astype(jnp.bfloat16)
         marks = jnp.where(same_row & (digit_in == 6), 1.0, 0.0).astype(jnp.bfloat16)
+        row_lane = lax.broadcasted_iota(jnp.int32, (span, head_width), 1) // 8
+        down_stats = 0.0
+        for row in range(rows):
+            spread = jnp.dot(
+                spread_moves[row], down_stats_into[chunk], preferred_element_type=jnp.float32
+            )
+            down_stats = down_stats + jnp.where(row_lane == row, spread, 0.0)
         levels = []
-        for ref in (own_stats, up_stats_into, down_stats_into):
-            stat = ref[chunk]
+        for stat in (own_stats[chunk], up_stats_into[chunk], down_stats.astype(jnp.bfloat16)):
             level = jnp.dot(stat, gather, preferred_element_type=jnp.float32)
             present = jnp.dot(stat, marks, preferred_element_type=jnp.float32)
             levels.append(jnp.where(present > 0.5, level, jnp.float32(-3e30)))
@@ -456,11 +466,14 @@
         norm = 1.0 / (shares[0] + shares[1] + shares[2])
         shares = [share * norm for share in shares]
         for row in range(rows):
+            spread = jnp.dot(
+                spread_moves[row], down_into[chunk, row], preferred_element_type=jnp.float32
+            )
             for head in range(2):
                 lanes = slice(head * head_width, (head + 1) * head_width)
                 lane = row * 8 + head * 3
-                value = 0.0
-                for part, share in zip((own, up_into, down_into), shares):
+                value = spread[:, lanes] * shares[2][:, lane : lane + 1]
+                for part, share in zip((own, up_into), shares):
                     value = value + part[chunk, row, :, lanes].astype(jnp.float32) * share[:, lane : lane + 1]
                 value = value.astype(jnp.bfloat16)
                 column = pl.multiple_of((2 * head + side) * head_width, head_width)
@@ -636,8 +649,10 @@
             vmem(chunks, 3, rows, span, wide),
             vmem(*context),
             vmem(chunks, rows, 2 * span, wide + head_width),
-            *[vmem(*context)] * 5,
-            *[vmem(*stats)] * 5,
+            *[vmem(*context)] * 3,
+            *[vmem(chunks, rows, span // 2, wide)] * 2,
+            *[vmem(*stats)] * 3,
+            *[vmem(chunks, span // 2, head_width)] * 2,
             vmem(planes, halves, weight_rows, 2 * part),
             vmem(chunks, members, rows * piece, 2 * wide),
             pltpu.VMEM((halves, members, rows * piece, 2 * part), jnp.float32),
@@ -645,7 +660,8 @@
             vmem(halves, members, rows * piece, 2 * part),
             vmem(rows, span, 2 * span),
             vmem(rows, span, 2 * span),
-            vmem(rows, span, span),
+            vmem(rows, span // 2, span),
+            vmem(rows, span, span // 2),
             pltpu.VMEM((rows, span, span), jnp.float32),
             pltpu.VMEM((rows, span, span), jnp.float32),
             dma((chunks,)),

time: 172 us -> 170 us (0.988)
  the two profiles are of different devices: /device:TPU:0 before, /device:TPU:26 now
where the time goes in v7:
time: 170 us; the launch traced here: 169 us
  Pallas kernels  164 us (96%)
  local copies, waits for them, and re-layouts  5.12 us (3%)
    pallas_call x1, Pallas kernels, fused_body(): pl.pallas_call(functools.partial(pair_kernel, geometry), out_shape=jax.Sh...  164 us

profile of v7, /device:TPU:26, one launch (start us, length us, event | category | flops | bytes accessed | tf_op | source)
XLA Modules:
  0.0 169.3 jit_solution(8567825983680723212)
XLA Ops:
  0.0 1.9 %copy.9 = bf16[512,1,2,2,256]{4,3,1,0,2:T(2,128)(2,1)S(1)} copy(bf16[512,1,2,2,256]{4,3,2,1,0:T(2,128)(2,1)} %bitcast.8) | data formatting | bytes 2097152 | tf_op jit(solution)/shard_map/reshape | solution.py:634
  1.9 1.5 reshape.7.weight_ref
  3.5 164.2 %shard_map.55 = bf16[4,64,512]{2,1,0:T(8,128)(2,1)} custom-call(s32[4,64]{1,0:T(4,128)} %lengths_ref.1, bf16[1,4,64,4096]{3,2,1,0:T(8,128)(2,1)} %q_ref.1, bf16[1,4,64,4096]{3,2,1,0:T(8,128)(2,1)} %k_ref.1, bf16[1,4,64,4096]{3,2,1,0:T(8,128)(2,1)} %v_ref.1, bf16[2,512,512]{2,1,0:T(8,128)(2,1)} %reshape.7.weight_ref), custom_call_target="tpu_custom_call" | custom-call | tf_op jit(solution)/shard_map/pallas_call | solution.py:643
  167.7 1.7 copy.11
